TPU v7x, 256 devices: a whole 4x4x8 slice. The times are simulated.
256 devices in a mesh: blk: 16 (over y_hi, x, core), head: 16 (over z, y_lo).
Axes of the slice: x: 4, y: 4 (y_hi: 2, y_lo: 2; y = y_hi * 2 + y_lo), z: 8, core: 2. Of those that a mesh axis runs over, the one named last changes fastest.
Arguments:
- queries: bfloat16 [32768, 4096], P(('blk', 'head')), may hold values from -6 to 6
- key_matrix: bfloat16 [32768, 512], P(('blk', 'head')), may hold values from -6 to 6
- value_matrix: bfloat16 [32768, 512], P(('blk', 'head')), may hold values from -6 to 6
- saved_output: bfloat16 [32768, 4096], P(('blk', 'head')), may hold values from -4 to 4
- output_gradient: bfloat16 [32768, 4096], P(('blk', 'head')), may hold values from -96 to 96
- saved_logsumexp: float32 [32768, 32], P(('blk', 'head')), may hold values from -1 to 16
- block_order: int32 [32], replicated, may hold values from 0 to 31, as said below
Outputs:
- query_grad: float32 [32768, 4096], P(('blk', 'head'))
- key_gradient: float32 [32768, 512], P(('blk', 'head'))
- value_gradient: float32 [32768, 512], P(('blk', 'head'))
Inputs may be any that keep to these rules, and one draw needn't show every extreme that they name: `block_order`: a permutation of 0 to 31.
All inputs are finite; a program needn't handle non-finite values.
Results may differ from a plain program's by a relative error of at most 0.0028.
Values may be sent and summed in bfloat16 or wider, within the bound.
A program may use at most 192 MiB of HBM per device.

v0:
```python
import jax
import jax.numpy as jnp
from jax import lax
from jax.sharding import PartitionSpec as P

HEAD_FEATURES = 128
WINDOW_ROUNDS = 2


def passed_along(block, axis, distance):
    devices = range(lax.axis_size(axis))
    route = [((i - distance) % len(devices), i) for i in devices]
    return lax.ppermute(block, axis, route)


def block_positions(block_order, block_id, seg_len):
    starts = lax.dynamic_slice(block_order, (2 * block_id,), (2,))
    offsets = jnp.arange(seg_len, dtype=jnp.int32)
    return (starts[:, None] * seg_len + offsets[None, :]).reshape(2 * seg_len)


def segment_positions(block_order, seg_id, seg_len):
    start = lax.dynamic_slice(block_order, (seg_id,), (1,))
    return start * seg_len + jnp.arange(seg_len, dtype=jnp.int32)


def widen_heads(rows_in, kv_heads, copies):
    tok_count = rows_in.shape[0]
    spread = jnp.broadcast_to(
        rows_in.reshape(tok_count, kv_heads, 1, HEAD_FEATURES),
        (tok_count, kv_heads, copies, HEAD_FEATURES),
    )
    return spread.reshape(tok_count, kv_heads * copies * HEAD_FEATURES)


def body(
    queries, key_matrix, value_matrix, saved_output, output_gradient, saved_logsumexp, block_order
):
    head_count = lax.axis_size("head")
    block_count = lax.axis_size("blk")
    tok_count = queries.shape[0]
    kv_heads = key_matrix.shape[1] // HEAD_FEATURES
    copies = max(1, head_count // kv_heads)
    key_wide = widen_heads(key_matrix, kv_heads, copies)
    value_wide = widen_heads(value_matrix, kv_heads, copies)
    local_query, local_dout, local_key, local_value, local_out = (
        lax.all_to_all(queries, "head", split_axis=1, concat_axis=0, tiled=True),
        lax.all_to_all(output_gradient, "head", split_axis=1, concat_axis=0, tiled=True),
        lax.all_to_all(key_wide, "head", split_axis=1, concat_axis=0, tiled=True),
        lax.all_to_all(value_wide, "head", split_axis=1, concat_axis=0, tiled=True),
        lax.all_to_all(saved_output, "head", split_axis=1, concat_axis=0, tiled=True),
    )
    local_lse = lax.all_to_all(saved_logsumexp, "head", split_axis=1, concat_axis=0, tiled=True)
    gathered = local_query.shape[0]
    local_delta = jnp.sum(
        (local_dout.astype(jnp.float32) * local_out.astype(jnp.float32)).reshape(
            gathered, -1, HEAD_FEATURES
        ),
        axis=2,
    )
    row_count = local_query.shape[0]
    seg_len = row_count // 2
    heads_dev = local_query.shape[1] // HEAD_FEATURES
    kv_dev = local_key.shape[1] // HEAD_FEATURES
    per_kv = heads_dev // kv_dev
    scaling = HEAD_FEATURES ** (-0.5)
    query4 = local_query.reshape(row_count, kv_dev, per_kv, HEAD_FEATURES)
    dout4 = local_dout.reshape(row_count, kv_dev, per_kv, HEAD_FEATURES)
    lse_heads = local_lse.reshape(row_count, kv_dev, per_kv).transpose(1, 2, 0)
    delta_heads = local_delta.reshape(row_count, kv_dev, per_kv).transpose(1, 2, 0)
    my_block = lax.axis_index("blk")
    query_pos = block_positions(block_order, my_block, seg_len)
    key_block, value_block = (local_key, local_value)
    query_acc = jnp.zeros((row_count, heads_dev * HEAD_FEATURES), jnp.float32)
    key_acc = jnp.zeros((row_count, kv_dev * HEAD_FEATURES), jnp.float32)
    value_acc = jnp.zeros((row_count, kv_dev * HEAD_FEATURES), jnp.float32)
    for round_index in range(WINDOW_ROUNDS):
        half = round_index % 2
        if round_index % 2 == 1:
            key_block, value_block = passed_along((key_block, value_block), "blk", 1)
            key_acc, value_acc = passed_along((key_acc, value_acc), "blk", 1)
        seg_id = (2 * my_block - round_index) % (2 * block_count)
        lower = half * seg_len
        key_seg = key_block[lower : lower + seg_len]
        value_seg = value_block[lower : lower + seg_len]
        key_pos = segment_positions(block_order, seg_id, seg_len)
        key3 = key_seg.reshape(seg_len, kv_dev, HEAD_FEATURES)
        value3 = value_seg.reshape(seg_len, kv_dev, HEAD_FEATURES)
        causal = query_pos[:, None] >= key_pos[None, :]
        scores = (
            jnp.einsum("qcgd,kcd->cgqk", query4, key3, preferred_element_type=jnp.float32) * scaling
        )
        weights = jnp.where(causal, jnp.exp(scores - lse_heads[..., None]), 0.0)
        prob_grad = jnp.einsum("qcgd,kcd->cgqk", dout4, value3, preferred_element_type=jnp.float32)
        score_grad = weights * (prob_grad - delta_heads[..., None])
        weights_low = weights.astype(jnp.bfloat16)
        grad_low = score_grad.astype(jnp.bfloat16)
        value_partial = jnp.einsum(
            "cgqk,qcgd->kcd", weights_low, dout4, preferred_element_type=jnp.float32
        )
        key_partial = (
            jnp.einsum("cgqk,qcgd->kcd", grad_low, query4, preferred_element_type=jnp.float32)
            * scaling
        )
        query_part = (
            jnp.einsum("cgqk,kcd->qcgd", grad_low, key3, preferred_element_type=jnp.float32)
            * scaling
        )
        query_part, key_partial, value_partial = (
            query_part.reshape(row_count, heads_dev * HEAD_FEATURES),
            key_partial.reshape(seg_len, kv_dev * HEAD_FEATURES),
            value_partial.reshape(seg_len, kv_dev * HEAD_FEATURES),
        )
        query_acc = query_acc + query_part
        key_acc = key_acc.at[lower : lower + seg_len].add(key_partial)
        value_acc = value_acc.at[lower : lower + seg_len].add(value_partial)
    key_acc, value_acc = passed_along((key_acc, value_acc), "blk", -(WINDOW_ROUNDS // 2))
    query_home, key_home, value_home = (
        lax.all_to_all(query_acc, "head", split_axis=0, concat_axis=1, tiled=True),
        lax.all_to_all(key_acc, "head", split_axis=0, concat_axis=1, tiled=True),
        lax.all_to_all(value_acc, "head", split_axis=0, concat_axis=1, tiled=True),
    )
    key_gradient = jnp.sum(
        key_home.reshape(tok_count, kv_heads, copies, HEAD_FEATURES), axis=2
    ).reshape(tok_count, kv_heads * HEAD_FEATURES)
    value_gradient = jnp.sum(
        value_home.reshape(tok_count, kv_heads, copies, HEAD_FEATURES), axis=2
    ).reshape(tok_count, kv_heads * HEAD_FEATURES)
    return (query_home, key_gradient, value_gradient)


def solution(mesh):
    return jax.shard_map(
        body,
        mesh=mesh,
        in_specs=(
            P(("blk", "head"), None),
            P(("blk", "head"), None),
            P(("blk", "head"), None),
            P(("blk", "head"), None),
            P(("blk", "head"), None),
            P(("blk", "head"), None),
            P(),
        ),
        out_specs=(P(("blk", "head"), None), P(("blk", "head"), None), P(("blk", "head"), None)),
        check_vma=False,
    )
```

profile of v0, /device:TPU:7, one launch (start us, length us, event | category | flops | bytes accessed | tf_op | source)
XLA Modules:
  0.0 351.0 jit_solution(17551969578027265312)
XLA Ops:
  2.5 9.4 %all-to-all-start.3 = ((bf16[128,16,128]{2,0,1:T(8,128)(2,1)}), bf16[128,16,128]{2,0,1:T(8,128)(2,1)}, u32[]{:S(2)}, u32[]{:S(2)}) async-start(bf16[128,16,128]{2,0,1:T(8,128)(2,1)} %bitcast.14), calls=%async_computation.3 | async-start | bytes 1048576 | tf_op jit(solution)/shard_map/all_to_all | solution.py:50
  12.8 14.7 %all-to-all-done.3 = bf16[128,16,128]{2,0,1:T(8,128)(2,1)} async-done(((bf16[128,16,128]{2,0,1:T(8,128)(2,1)}), bf16[128,16,128]{2,0,1:T(8,128)(2,1)}, u32[]{:S(2)}, u32[]{:S(2)}) %all-to-all-start.3) | async-done | bytes 524320 | tf_op jit(solution)/shard_map/all_to_all | solution.py:50
  28.4 4.8 %all-to-all-start = ((bf16[128,16,128]{2,0,1:T(8,128)(2,1)}), bf16[128,16,128]{2,0,1:T(8,128)(2,1)}, u32[]{:S(2)}, u32[]{:S(2)}) async-start(bf16[128,16,128]{2,0,1:T(8,128)(2,1)} %bitcast.1), calls=%async_computation | async-start | bytes 1048576 | tf_op jit(solution)/shard_map/all_to_all | solution.py:49
  33.3 2.3 copy.70
  35.5 12.8 %all-to-all-done = bf16[128,16,128]{2,0,1:T(8,128)(2,1)} async-done(((bf16[128,16,128]{2,0,1:T(8,128)(2,1)}), bf16[128,16,128]{2,0,1:T(8,128)(2,1)}, u32[]{:S(2)}, u32[]{:S(2)}) %all-to-all-start) | async-done | bytes 524320 | tf_op jit(solution)/shard_map/all_to_all | solution.py:49
  48.3 4.2 %all-to-all-start.1 = ((bf16[128,16,256]{0,2,1:T(8,128)(2,1)}), bf16[128,16,256]{0,2,1:T(8,128)(2,1)S(1)}, u32[]{:S(2)}, u32[]{:S(2)}) async-start(bf16[128,16,256]{0,2,1:T(8,128)(2,1)} %bitcast.5), calls=%async_computation.1 | async-start | bytes 2097152 | tf_op jit(solution)/shard_map/all_to_all | solution.py:47
  52.5 1.3 copy.77
  53.8 23.1 %all-to-all-done.1 = bf16[128,16,256]{0,2,1:T(8,128)(2,1)S(1)} async-done(((bf16[128,16,256]{0,2,1:T(8,128)(2,1)}), bf16[128,16,256]{0,2,1:T(8,128)(2,1)S(1)}, u32[]{:S(2)}, u32[]{:S(2)}) %all-to-all-start.1) | async-done | bytes 1048608 | tf_op jit(solution)/shard_map/all_to_all | solution.py:47
  76.9 7.2 %all-to-all-start.5 = ((bf16[128,16,256]{0,2,1:T(8,128)(2,1)}), bf16[128,16,256]{0,2,1:T(8,128)(2,1)S(1)}, u32[]{:S(2)}, u32[]{:S(2)}) async-start(bf16[128,16,256]{0,2,1:T(8,128)(2,1)} %bitcast.22), calls=%async_computation.5 | async-start | bytes 2097152 | tf_op jit(solution)/shard_map/all_to_all | solution.py:51
  84.1 1.3 copy.74
  85.5 24.2 %all-to-all-done.5 = bf16[128,16,256]{0,2,1:T(8,128)(2,1)S(1)} async-done(((bf16[128,16,256]{0,2,1:T(8,128)(2,1)}), bf16[128,16,256]{0,2,1:T(8,128)(2,1)S(1)}, u32[]{:S(2)}, u32[]{:S(2)}) %all-to-all-start.5) | async-done | bytes 1048608 | tf_op jit(solution)/shard_map/all_to_all | solution.py:51
  109.6 6.2 %all-to-all-start.4 = ((bf16[128,16,256]{0,2,1:T(8,128)(2,1)}), bf16[128,16,256]{0,2,1:T(8,128)(2,1)}, u32[]{:S(2)}, u32[]{:S(2)}) async-start(bf16[128,16,256]{0,2,1:T(8,128)(2,1)} %bitcast.18), calls=%async_computation.4 | async-start | bytes 2097152 | tf_op jit(solution)/shard_map/all_to_all | solution.py:48
  118.0 3.7 %broadcast_compare_fusion = (pred[2048,1024]{0,1:T(8,128)(4,1)}, pred[2048,1024]{0,1:T(8,128)(4,1)}) fusion(s32[2048]{0:T(1024)S(1)} %bitcast.210, s32[1024]{0:T(1024)S(1)} %get-tuple-element.64, s32[1024]{0:T(1024)S(1)} %get-tuple-element.65), kind=kLoop, calls=%fused_computation.22 | loop fusion | flops 4194304 | bytes 4210688 | tf_op jit(solution)/shard_map/ge | solution.py:89
  121.6 1.7 slice.91
  124.3 4.8 %collective-permute-start = (bf16[2048,128]{1,0:T(8,128)(2,1)}, bf16[2048,128]{1,0:T(8,128)(2,1)}, u32[]{:S(2)}, u32[]{:S(2)}) collective-permute-start(bf16[2048,128]{1,0:T(8,128)(2,1)} %bitcast.29), channel_id=1, source_target_pairs={{240,0},{0,16},{16,32},{32,48},{48,64},{64,80},{80,96},{96,112},{1... | collective-permute-start | bytes 1572872 | tf_op jit(solution)/shard_map/ppermute | solution.py:13
  130.5 2.5 copy.78
  133.1 1.7 reshape.300
  134.8 5.5 %all-to-all-done.4 = bf16[128,16,256]{0,2,1:T(8,128)(2,1)} async-done(((bf16[128,16,256]{0,2,1:T(8,128)(2,1)}), bf16[128,16,256]{0,2,1:T(8,128)(2,1)}, u32[]{:S(2)}, u32[]{:S(2)}) %all-to-all-start.4) | async-done | bytes 1048608 | tf_op jit(solution)/shard_map/all_to_all | solution.py:48
  140.3 7.7 %all-to-all-start.2 = ((f32[128,16,2]{0,2,1:T(2,128)}), f32[128,16,2]{0,2,1:T(2,128)S(1)}, u32[]{:S(2)}, u32[]{:S(2)}) async-start(f32[128,16,2]{0,2,1:T(2,128)} %bitcast.9), calls=%async_computation.2 | async-start | bytes 32768 | tf_op jit(solution)/shard_map/all_to_all | solution.py:53
  148.0 2.9 copy.75
  150.9 2.3 reshape.290
  153.2 8.1 %fusion.40 = f32[1024,2048,2]{1,0,2:T(8,128)} fusion(bf16[1024,128,1]{1,0,2:T(8,128)(2,1)S(1)} %bitcast.204, bf16[2048,2,128]{0,2,1:T(8,128)(2,1)S(1)} %reshape.287), kind=kOutput, calls=%fused_computation.56 | convolution fusion | flops 1073741824 | bytes 18087936 | tf_op jit(solution)/shard_map/qcgd,kcd->cgqk/dot_general | solution.py:91
  161.6 12.0 %fusion.12 = bf16[2,2048,1024]{1,2,0:T(8,128)(2,1)S(1)} fusion(f32[1024,2048,2]{1,0,2:T(8,128)} %fusion.40, f32[2,2048]{1,0:T(2,128)S(1)} %bitcast.211, f32[2,2048]{1,0:T(2,128)S(1)} %bitcast.213, pred[2048,1024]{0,1:T(8,128)(4,1)} %get-tuple-element.61, bf16[1024,128,1]{1,0,2:T(8,128)(2,1)} %bitcast.209, bf16[2048,2,128]{0,2,1:T(8,128)(2,1)} %reshape.290), kind=kOutput, calls=%fused_computation.16 | convolution fusion | flops 1098907648 | bytes 28606464 | tf_op jit(solution)/shard_map/qcgd,kcd->cgqk/dot_general | solution.py:94
  173.6 9.2 %fusion.32 = f32[1024,2048,2]{1,0,2:T(8,128)} fusion(bf16[2048,2,128]{0,2,1:T(8,128)(2,1)S(1)} %reshape.287, bf16[2048,128]{1,0:T(8,128)(2,1)} %collective-permute-done), kind=kOutput, calls=%fused_computation.43 | convolution fusion | flops 1073741824 | bytes 18087936 | tf_op jit(solution)/shard_map/qcgd,kcd->cgqk/dot_general | solution.py:91
  182.8 2.4 fusion.41
  185.3 9.5 %fusion.13 = bf16[2,2048,1024]{1,2,0:T(8,128)(2,1)S(1)} fusion(f32[1024,2048,2]{1,0,2:T(8,128)} %fusion.32, f32[2,2048]{1,0:T(2,128)S(1)} %bitcast.212, f32[2,2048]{1,0:T(2,128)S(1)} %bitcast.214, pred[2048,1024]{0,1:T(8,128)(4,1)} %get-tuple-element.60, bf16[2048,2,128]{0,2,1:T(8,128)(2,1)S(1)} %copy-done.5, bf16[2048,128]{1,0:T(8,128)(2,1)} %collective-permute-done.1), kind=kOutput, calls=%fused_computation.17 | convolution fusion | flops 1098907648 | bytes 28606464 | tf_op jit(solution)/shard_map/qcgd,kcd->cgqk/dot_general | solution.py:94
  194.8 3.2 copy-done.2
  198.0 3.3 fusion.21
  201.4 1.8 copy.83
  203.2 2.0 copy.107
  205.2 2.0 copy.84
  207.2 7.6 %all-to-all-start.6 = ((f32[16,128,256]{1,2,0:T(8,128)}), f32[16,128,256]{1,2,0:T(8,128)S(1)}, u32[]{:S(2)}, u32[]{:S(2)}) async-start(f32[16,128,256]{1,2,0:T(8,128)} %copy.84), calls=%async_computation.6 | async-start | bytes 4194304 | tf_op jit(solution)/shard_map/all_to_all | solution.py:119
  214.8 8.5 %fusion.27 = f32[1024,128]{1,0:T(8,128)S(1)} fusion(bf16[2048,2,128]{0,2,1:T(8,128)(2,1)} %reshape.290, f32[1024,2048,2]{1,0,2:T(8,128)} %fusion.40, f32[2,2048]{1,0:T(2,128)S(1)} %bitcast.215, pred[2048,1024]{0,1:T(8,128)(4,1)} %get-tuple-element.61), kind=kOutput, calls=%fused_computation.34 | convolution fusion | flops 1090519040 | bytes 20463616 | tf_op jit(solution)/shard_map/cgqk,qcgd->kcd/dot_general | solution.py:98
  223.4 9.1 %collective-permute-start.4 = (f32[2048,128]{1,0:T(8,128)S(1)}, f32[2048,128]{1,0:T(8,128)}, u32[]{:S(2)}, u32[]{:S(2)}) collective-permute-start(f32[2048,128]{1,0:T(8,128)S(1)} %scatter-add.16), channel_id=1, source_target_pairs={{240,0},{0,16},{16,32},{32,48},{48,64},{64,80},{80,96},{96,112},{1... | collective-permute-start | bytes 3145736 | tf_op jit(solution)/shard_map/ppermute | solution.py:13
  232.6 14.2 %collective-permute-done.4 = f32[2048,128]{1,0:T(8,128)} collective-permute-done((f32[2048,128]{1,0:T(8,128)S(1)}, f32[2048,128]{1,0:T(8,128)}, u32[]{:S(2)}, u32[]{:S(2)}) %collective-permute-start.4) | collective-permute-done | bytes 1048608 | tf_op jit(solution)/shard_map/ppermute | solution.py:13
  246.8 8.9 %fusion.30 = f32[2048,128]{1,0:T(8,128)} fusion(f32[2048,128]{1,0:T(8,128)} %collective-permute-done.4, bf16[2048,2,128]{0,2,1:T(8,128)(2,1)S(1)} %copy-done.6, f32[1024,2048,2]{1,0,2:T(8,128)} %fusion.32, f32[2,2048]{1,0:T(2,128)S(1)} %bitcast.216, pred[2048,1024]{0,1:T(8,128)(4,1)S(1)} %copy-done.7), kind=kOutput, calls=%fused_computation.38 | convolution fusion | flops 1090650112 | bytes 20987904 | tf_op jit(solution)/shard_map/cgqk,qcgd->kcd/dot_general | solution.py:98
  256.0 2.4 fusion.23
  258.3 1.0 scatter-add.14
  259.4 8.9 %collective-permute-start.2 = (f32[2048,128]{1,0:T(8,128)}, f32[2048,128]{1,0:T(8,128)}, u32[]{:S(2)}, u32[]{:S(2)}) collective-permute-start(f32[2048,128]{1,0:T(8,128)} %scatter-add.14), channel_id=1, source_target_pairs={{240,0},{0,16},{16,32},{32,48},{48,64},{64,80},{80,96},{96,112},{1... | collective-permute-start | bytes 3145736 | tf_op jit(solution)/shard_map/ppermute | solution.py:13
  268.3 9.6 %collective-permute-done.5 = f32[2048,128]{1,0:T(8,128)} collective-permute-done((f32[2048,128]{1,0:T(8,128)}, f32[2048,128]{1,0:T(8,128)}, u32[]{:S(2)}, u32[]{:S(2)}) %collective-permute-start.5) | collective-permute-done | bytes 1048608 | tf_op jit(solution)/shard_map/ppermute | solution.py:13
  277.9 16.5 %all-to-all-start.8 = ((f32[16,128,128]{2,1,0:T(8,128)}), f32[16,128,128]{2,1,0:T(8,128)}, u32[]{:S(2)}, u32[]{:S(2)}) async-start(f32[16,128,128]{2,1,0:T(8,128)} %bitcast.53), calls=%async_computation.8 | async-start | bytes 2097152 | tf_op jit(solution)/shard_map/all_to_all | solution.py:121
  294.5 6.6 %fusion.31 = f32[2048,128]{1,0:T(8,128)} fusion(f32[2048,128]{1,0:T(8,128)} %collective-permute-done.2, bf16[2,2048,1024]{1,2,0:T(8,128)(2,1)} %copy-done.2, bf16[2048,2,128]{0,2,1:T(8,128)(2,1)S(1)} %reshape.287), kind=kOutput, calls=%fused_computation.40 | convolution fusion | flops 1074003968 | bytes 10485760 | tf_op jit(solution)/shard_map/cgqk,qcgd->kcd/dot_general | solution.py:102
  301.1 20.4 %collective-permute-done.3 = f32[2048,128]{1,0:T(8,128)S(1)} collective-permute-done((f32[2048,128]{1,0:T(8,128)}, f32[2048,128]{1,0:T(8,128)S(1)}, u32[]{:S(2)}, u32[]{:S(2)}) %collective-permute-start.3) | collective-permute-done | bytes 1048608 | tf_op jit(solution)/shard_map/ppermute | solution.py:13
  321.5 1.0 copy-done.10
  322.5 10.1 %all-to-all-start.7 = ((f32[16,128,128]{2,1,0:T(8,128)}), f32[16,128,128]{2,1,0:T(8,128)S(1)}, u32[]{:S(2)}, u32[]{:S(2)}) async-start(f32[16,128,128]{2,1,0:T(8,128)} %bitcast.206), calls=%async_computation.7 | async-start | bytes 2097152 | tf_op jit(solution)/shard_map/all_to_all | solution.py:120
  332.7 1.8 copy.91
  334.5 1.3 bitcast_reduce_fusion
  336.8 13.0 %all-to-all-done.7 = f32[16,128,128]{2,1,0:T(8,128)S(1)} async-done(((f32[16,128,128]{2,1,0:T(8,128)}), f32[16,128,128]{2,1,0:T(8,128)S(1)}, u32[]{:S(2)}, u32[]{:S(2)}) %all-to-all-start.7) | async-done | bytes 1048608 | tf_op jit(solution)/shard_map/all_to_all | solution.py:120
  (56 shorter events, 9.4 us)
Async XLA Ops:
  0.6 0.9 copy-start
  0.6 51.9 %copy-start.8 = (bf16[128,4096]{1,0:T(8,128)(2,1)S(1)}, bf16[128,4096]{1,0:T(8,128)(2,1)}, u32[]{:S(2)}) copy-start(bf16[128,4096]{1,0:T(8,128)(2,1)} %param.18) | copy-start | bytes 3145732
  0.7 83.5 %copy-start.9 = (bf16[128,4096]{1,0:T(8,128)(2,1)S(1)}, bf16[128,4096]{1,0:T(8,128)(2,1)}, u32[]{:S(2)}) copy-start(bf16[128,4096]{1,0:T(8,128)(2,1)} %param.19) | copy-start | bytes 3145732
  0.7 115.2 %copy-start.11 = (s32[32]{0:T(128)S(1)}, s32[32]{0:T(128)}, u32[]{:S(2)}) copy-start(s32[32]{0:T(128)} %param.21) | copy-start | bytes 388
  2.5 25.0 %all-to-all-start.3 = ((bf16[128,16,128]{2,0,1:T(8,128)(2,1)}), bf16[128,16,128]{2,0,1:T(8,128)(2,1)}, u32[]{:S(2)}, u32[]{:S(2)}) async-start(bf16[128,16,128]{2,0,1:T(8,128)(2,1)} %bitcast.14), calls=%async_computation.3 | async-start | bytes 1048576 | tf_op jit(solution)/shard_map/all_to_all | solution.py:50
  28.4 19.9 %all-to-all-start = ((bf16[128,16,128]{2,0,1:T(8,128)(2,1)}), bf16[128,16,128]{2,0,1:T(8,128)(2,1)}, u32[]{:S(2)}, u32[]{:S(2)}) async-start(bf16[128,16,128]{2,0,1:T(8,128)(2,1)} %bitcast.1), calls=%async_computation | async-start | bytes 1048576 | tf_op jit(solution)/shard_map/all_to_all | solution.py:49
  48.3 28.6 %all-to-all-start.1 = ((bf16[128,16,256]{0,2,1:T(8,128)(2,1)}), bf16[128,16,256]{0,2,1:T(8,128)(2,1)S(1)}, u32[]{:S(2)}, u32[]{:S(2)}) async-start(bf16[128,16,256]{0,2,1:T(8,128)(2,1)} %bitcast.5), calls=%async_computation.1 | async-start | bytes 2097152 | tf_op jit(solution)/shard_map/all_to_all | solution.py:47
  76.9 32.7 %all-to-all-start.5 = ((bf16[128,16,256]{0,2,1:T(8,128)(2,1)}), bf16[128,16,256]{0,2,1:T(8,128)(2,1)S(1)}, u32[]{:S(2)}, u32[]{:S(2)}) async-start(bf16[128,16,256]{0,2,1:T(8,128)(2,1)} %bitcast.22), calls=%async_computation.5 | async-start | bytes 2097152 | tf_op jit(solution)/shard_map/all_to_all | solution.py:51
  109.6 30.7 %all-to-all-start.4 = ((bf16[128,16,256]{0,2,1:T(8,128)(2,1)}), bf16[128,16,256]{0,2,1:T(8,128)(2,1)}, u32[]{:S(2)}, u32[]{:S(2)}) async-start(bf16[128,16,256]{0,2,1:T(8,128)(2,1)} %bitcast.18), calls=%async_computation.4 | async-start | bytes 2097152 | tf_op jit(solution)/shard_map/all_to_all | solution.py:48
  124.3 49.3 %collective-permute-start = (bf16[2048,128]{1,0:T(8,128)(2,1)}, bf16[2048,128]{1,0:T(8,128)(2,1)}, u32[]{:S(2)}, u32[]{:S(2)}) collective-permute-start(bf16[2048,128]{1,0:T(8,128)(2,1)} %bitcast.29), channel_id=1, source_target_pairs={{240,0},{0,16},{16,32},{32,48},{48,64},{64,80},{80,96},{96,112},{1... | collective-permute-start | bytes 1572872 | tf_op jit(solution)/shard_map/ppermute | solution.py:13
  129.1 56.2 %collective-permute-start.1 = (bf16[2048,128]{1,0:T(8,128)(2,1)}, bf16[2048,128]{1,0:T(8,128)(2,1)}, u32[]{:S(2)}, u32[]{:S(2)}) collective-permute-start(bf16[2048,128]{1,0:T(8,128)(2,1)} %bitcast.33), channel_id=1, source_target_pairs={{240,0},{0,16},{16,32},{32,48},{48,64},{64,80},{80,96},{96,112},{1... | collective-permute-start | bytes 1572872 | tf_op jit(solution)/shard_map/ppermute | solution.py:13
  140.3 21.3 %all-to-all-start.2 = ((f32[128,16,2]{0,2,1:T(2,128)}), f32[128,16,2]{0,2,1:T(2,128)S(1)}, u32[]{:S(2)}, u32[]{:S(2)}) async-start(f32[128,16,2]{0,2,1:T(2,128)} %bitcast.9), calls=%async_computation.2 | async-start | bytes 32768 | tf_op jit(solution)/shard_map/all_to_all | solution.py:53
  153.2 8.1 %copy-start.4 = (bf16[2048,2,128]{0,2,1:T(8,128)(2,1)S(1)}, bf16[2048,2,128]{0,2,1:T(8,128)(2,1)}, u32[]{:S(2)}) copy-start(bf16[2048,2,128]{0,2,1:T(8,128)(2,1)} %reshape.290) | copy-start | bytes 3145732
  173.5 9.3 %copy-start.3 = (bf16[2,2048,1024]{1,2,0:T(8,128)(2,1)}, bf16[2,2048,1024]{1,2,0:T(8,128)(2,1)S(1)}, u32[]{:S(2)}) copy-start(bf16[2,2048,1024]{1,2,0:T(8,128)(2,1)S(1)} %fusion.12) | copy-start | bytes 25165828
  182.8 2.4 copy-start.5
  194.8 3.2 copy-start.2
  207.2 70.8 %all-to-all-start.6 = ((f32[16,128,256]{1,2,0:T(8,128)}), f32[16,128,256]{1,2,0:T(8,128)S(1)}, u32[]{:S(2)}, u32[]{:S(2)}) async-start(f32[16,128,256]{1,2,0:T(8,128)} %copy.84), calls=%async_computation.6 | async-start | bytes 4194304 | tf_op jit(solution)/shard_map/all_to_all | solution.py:119
  214.8 32.0 %copy-start.6 = (bf16[2048,2,128]{0,2,1:T(8,128)(2,1)S(1)}, bf16[2048,2,128]{0,2,1:T(8,128)(2,1)}, u32[]{:S(2)}) copy-start(bf16[2048,2,128]{0,2,1:T(8,128)(2,1)} %reshape.290) | copy-start | bytes 3145732
  214.8 32.0 %copy-start.7 = (pred[2048,1024]{0,1:T(8,128)(4,1)S(1)}, pred[2048,1024]{0,1:T(8,128)(4,1)}, u32[]{:S(2)}) copy-start(pred[2048,1024]{0,1:T(8,128)(4,1)} %get-tuple-element.60) | copy-start | bytes 6291460
  223.3 32.6 %slice-start = ((s8[8388608]{0:T(1024)(128)(4,1)}), s8[4194304]{0:T(1024)(128)(4,1)S(1)}, s32[]{:S(2)}) async-start(s8[8388608]{0:T(1024)(128)(4,1)} %bitcast.198), calls=%async_computation.9 | async-start | bytes 8388608
  223.4 32.6 %slice-start.1 = ((s8[8388608]{0:T(1024)(128)(4,1)}), s8[4194304]{0:T(1024)(128)(4,1)S(1)}, s32[]{:S(2)}) async-start(s8[8388608]{0:T(1024)(128)(4,1)} %bitcast.198), calls=%async_computation.10 | async-start | bytes 8388608
  223.4 23.4 %collective-permute-start.4 = (f32[2048,128]{1,0:T(8,128)S(1)}, f32[2048,128]{1,0:T(8,128)}, u32[]{:S(2)}, u32[]{:S(2)}) collective-permute-start(f32[2048,128]{1,0:T(8,128)S(1)} %scatter-add.16), channel_id=1, source_target_pairs={{240,0},{0,16},{16,32},{32,48},{48,64},{64,80},{80,96},{96,112},{1... | collective-permute-start | bytes 3145736 | tf_op jit(solution)/shard_map/ppermute | solution.py:13
  255.7 22.2 %collective-permute-start.5 = (f32[2048,128]{1,0:T(8,128)}, f32[2048,128]{1,0:T(8,128)}, u32[]{:S(2)}, u32[]{:S(2)}) collective-permute-start(f32[2048,128]{1,0:T(8,128)} %fusion.30), channel_id=1, source_target_pairs={{16,0},{32,16},{48,32},{64,48},{80,64},{96,80},{112,96},{128,112},... | collective-permute-start | bytes 3145736 | tf_op jit(solution)/shard_map/ppermute | solution.py:13
  259.4 35.1 %collective-permute-start.2 = (f32[2048,128]{1,0:T(8,128)}, f32[2048,128]{1,0:T(8,128)}, u32[]{:S(2)}, u32[]{:S(2)}) collective-permute-start(f32[2048,128]{1,0:T(8,128)} %scatter-add.14), channel_id=1, source_target_pairs={{240,0},{0,16},{16,32},{32,48},{48,64},{64,80},{80,96},{96,112},{1... | collective-permute-start | bytes 3145736 | tf_op jit(solution)/shard_map/ppermute | solution.py:13
  277.9 43.6 %all-to-all-start.8 = ((f32[16,128,128]{2,1,0:T(8,128)}), f32[16,128,128]{2,1,0:T(8,128)}, u32[]{:S(2)}, u32[]{:S(2)}) async-start(f32[16,128,128]{2,1,0:T(8,128)} %bitcast.53), calls=%async_computation.8 | async-start | bytes 2097152 | tf_op jit(solution)/shard_map/all_to_all | solution.py:121
  294.5 56.3 %copy-start.1 = (bf16[128,512]{1,0:T(8,128)(2,1)S(1)}, bf16[128,512]{1,0:T(8,128)(2,1)}, u32[]{:S(2)}) copy-start(bf16[128,512]{1,0:T(8,128)(2,1)} %param.17) | copy-start | bytes 393220
  301.1 20.5 %collective-permute-start.3 = (f32[2048,128]{1,0:T(8,128)}, f32[2048,128]{1,0:T(8,128)S(1)}, u32[]{:S(2)}, u32[]{:S(2)}) collective-permute-start(f32[2048,128]{1,0:T(8,128)} %fusion.31), channel_id=1, source_target_pairs={{16,0},{32,16},{48,32},{64,48},{80,64},{96,80},{112,96},{128,112},... | collective-permute-start | bytes 3145736 | tf_op jit(solution)/shard_map/ppermute | solution.py:13
  321.5 1.0 copy-start.10
  322.5 27.2 %all-to-all-start.7 = ((f32[16,128,128]{2,1,0:T(8,128)}), f32[16,128,128]{2,1,0:T(8,128)S(1)}, u32[]{:S(2)}, u32[]{:S(2)}) async-start(f32[16,128,128]{2,1,0:T(8,128)} %bitcast.206), calls=%async_computation.7 | async-start | bytes 2097152 | tf_op jit(solution)/shard_map/all_to_all | solution.py:120
where the time goes:
time: 358 us; the launch traced here: 351 us
  waiting for transfers between devices  138 us (39%)
  starting transfers between devices  97 us (27%)
  matrix products  70.9 us (20%)
  local copies, waits for them, and re-layouts  37.2 us (10%)
  other arithmetic  5.68 us (2%)
    ppermute x6, waiting for transfers between devices, passed_along(): return lax.ppermute(block, axis, route)  44.3 us
    all_to_all x1, waiting for transfers between devices, body(): lax.all_to_all(saved_output, 'head', split_axis=1, concat_axis=0, tiled=T...  24.2 us
    ppermute x6, starting transfers between devices, passed_along(): return lax.ppermute(block, axis, route)  23.1 us
    all_to_all x1, waiting for transfers between devices, body(): lax.all_to_all(queries, 'head', split_axis=1, concat_axis=0, tiled=True)  23.1 us
    dot_general x2, matrix products, body(): jnp.einsum('qcgd,kcd->cgqk', dout4, value3, preferred_element_type=jnp.fl...  21.5 us
    dot_general x2, matrix products, body(): jnp.einsum('cgqk,qcgd->kcd', weights_low, dout4, preferred_element_type=j...  17.4 us
    dot_general x2, matrix products, body(): jnp.einsum('qcgd,kcd->cgqk', query4, key3, preferred_element_type=jnp.flo...  17.3 us
    all_to_all x1, starting transfers between devices, body(): lax.all_to_all(value_acc, 'head', split_axis=0, concat_axis=1, tiled=True)  16.5 us
  transfers between devices with their start and end apart: 15, of which 9 were waited for; matrix products, arithmetic and copies ran while one was open for 25% of the time, Pallas kernels for 0%

commit v1 on v0

v1 whole, which is shorter than its diff:
```python
import functools

import jax
import jax.numpy as jnp
from jax import lax
from jax.experimental import pallas as pl
from jax.experimental.pallas import tpu as pltpu
from jax.sharding import PartitionSpec as P

F32 = jnp.float32
BF16 = jnp.bfloat16
FEAT = 128
SCALE = FEAT**-0.5
LOG2E = 1.4426950408889634
UNSEEN = 1e30
MESH = pl.DeviceIdType.MESH


def dot(a, b, ca, cb):
    return lax.dot_general(a, b, (((ca,), (cb,)), ((), ())), preferred_element_type=F32)


def span(start, size):
    return pl.ds(pl.multiple_of(start, size), size)


def kernel(
    order, q_hbm, k_hbm, v_hbm, o_hbm, do_hbm, lse_ref, dq_hbm, dk_hbm, dv_hbm,
    q_s, do_s, kv_s, o_full, do_full, st_own, st_s, aux, mask_s, ps, dss, dq_t, dkv,
    rs_in, rs_out, fin, dq_out, dq_in, dq_stage,
    sem_full, sem_ql, sem_qr, sem_qs, sem_st, sem_ar, sem_as, sem_gr, sem_gs, sem_rr, sem_rs,
    sem_fr, sem_fs, sem_dqr, sem_dqs, sem_out,
):
    b = lax.axis_index("blk")
    hd = lax.axis_index("head")
    z = hd // 2
    y = hd % 2
    yo = 1 - y
    partner = (b, 2 * z + yo)
    ring = ((b, (hd + 2) % 16), (b, (hd + 14) % 16))
    nxt = (b + 1) % 16
    prv = (b + 15) % 16
    first_half = z < 4

    barrier = pltpu.get_barrier_semaphore()
    peers = [partner, ring[0], ring[1], (nxt, hd), (prv, hd), (nxt, 2 * z + yo), (prv, 2 * z + yo)]
    for peer in peers:
        pl.semaphore_signal(barrier, inc=1, device_id=peer, device_id_type=MESH)

    def local_q(a, t):
        src, dst = ((q_hbm, q_s), (do_hbm, do_s))[t]

        def one(h, c):
            pltpu.make_async_copy(
                src.at[:, span((16 * y + 8 * a + h) * FEAT, FEAT)], dst.at[a, y, h], sem_ql.at[a, t]
            ).start()
            return c

        lax.fori_loop(0, 8, one, 0)

    full_o = pltpu.make_async_copy(o_hbm, o_full, sem_full.at[0])
    full_do = pltpu.make_async_copy(do_hbm, do_full, sem_full.at[1])
    full_o.start()
    full_do.start()
    for a in range(2):
        for t in range(2):
            local_q(a, t)
    pl.semaphore_wait(barrier, len(peers))

    def remote(src, dst, ss, rs, dev):
        return pltpu.make_async_remote_copy(
            src_ref=src, dst_ref=dst, send_sem=ss, recv_sem=rs, device_id=dev, device_id_type=MESH
        )

    bt = jnp.where(first_half, b, nxt)
    for a in range(2):
        for kv, ref in enumerate((k_hbm, v_hbm)):
            dst = kv_s.at[a, z, kv, span(y * FEAT, FEAT)]
            far = ref.at[:, span((2 * yo + a) * FEAT, FEAT)]
            near = ref.at[:, span((2 * y + a) * FEAT, FEAT)]
            remote(far, dst, sem_as.at[0, a, kv], sem_ar.at[a, kv, y], (bt, 2 * z + yo)).start()

            @pl.when(first_half)
            def _():
                pltpu.make_async_copy(near, dst, sem_ar.at[a, kv, y]).start()

            @pl.when(jnp.logical_not(first_half))
            def _():
                remote(near, dst, sem_as.at[1, a, kv], sem_ar.at[a, kv, y], (bt, hd)).start()

    for a in range(2):
        for t, (src, dst) in enumerate(((q_hbm, q_s), (do_hbm, do_s))):

            def one(h, c):
                remote(
                    src.at[:, span((16 * yo + 8 * a + h) * FEAT, FEAT)], dst.at[a, y, h],
                    sem_qs.at[a, t], sem_qr.at[a, t], partner,
                ).start()
                return c

            lax.fori_loop(0, 8, one, 0)

    def gather_copy(d, a, s):
        j = (z + 8 - s) % 8 if d == 0 else (z + s) % 8
        return remote(
            kv_s.at[a, j], kv_s.at[a, j], sem_gs.at[d, a, s], sem_gr.at[d, a, s], ring[d]
        )

    def gather_wait(d, a, s):
        gather_copy(d, a, s).wait_recv()

    for a in range(2):
        for kv in range(2):
            for half in range(2):
                place = kv_s.at[a, z, kv, pl.ds(half * FEAT, FEAT)]
                pltpu.make_async_copy(place, place, sem_ar.at[a, kv, half]).wait()
        for d in range(2):
            gather_copy(d, a, 0).start()

    full_o.wait()
    full_do.wait()
    lane = lax.broadcasted_iota(jnp.int32, (FEAT, FEAT), 1)
    aux[...] = jnp.zeros_like(aux)
    aux[:, 0:32] = lse_ref[...] * LOG2E
    stats = aux[...]
    for h in range(32):
        cols = slice(h * FEAT, (h + 1) * FEAT)
        product = o_full[:, cols].astype(F32) * do_full[:, cols].astype(F32)
        stats = jnp.where(lane == 32 + h, jnp.sum(product, axis=1, keepdims=True), stats)
    turned = stats.T
    st_own[0] = turned[0:32]
    st_own[1] = turned[32:64]
    st_send = remote(
        st_own.at[:, span(16 * yo, 16)], st_s.at[y], sem_st.at[0], sem_st.at[1], partner
    )
    st_send.start()
    st_s[y] = st_own[:, span(16 * y, 16)]

    key_row = lax.broadcasted_iota(jnp.int32, (256, 256), 0)
    query_row = lax.broadcasted_iota(jnp.int32, (256, 256), 1) % FEAT
    mask_s[0] = jnp.zeros((256, 256), F32)
    for slot in range(2):
        mask_s[1 + slot] = jnp.where(key_row > slot * FEAT + query_row, UNSEEN, 0.0)
    dq_t[...] = jnp.zeros_like(dq_t)

    own_a, own_b, before = order[2 * b], order[2 * b + 1], order[(2 * b + 31) % 32]
    query_seg = jnp.where(first_half, own_a, own_b)

    def penalty(j):
        inside = jnp.where(first_half, jnp.where(j <= z, 0.0, UNSEEN), jnp.where(own_b > own_a, 0.0, UNSEEN))
        return jnp.where(j >= 4, jnp.where(query_seg > before, 0.0, UNSEEN), inside)

    def pair_unit(a, src, s, add):
        chunks = ((z + 7 - s) % 8, (z + (s + 1) % 4) % 8)
        masked = jnp.where(jnp.logical_and(s == 3, first_half), 1 + src, 0)
        for c, j in enumerate(chunks):
            key, value = kv_s[a, j, 0], kv_s[a, j, 1]
            pen = penalty(j)
            for t in range(4):
                qr = q_s[a, src, 2 * t : 2 * t + 2].reshape(256, FEAT)
                dr = do_s[a, src, 2 * t : 2 * t + 2].reshape(256, FEAT)
                rows = [st_s[src, k, pl.ds(8 * a + 2 * t + i, 1)] for k in range(2) for i in range(2)]
                lse_row = jnp.concatenate(rows[0:2], axis=1) + pen
                delta_row = jnp.concatenate(rows[2:4], axis=1)
                x = dot(key, qr, 1, 1) * (SCALE * LOG2E) - lse_row
                if c == 1:
                    x = x - mask_s[masked]
                p = jnp.exp2(x)
                g = p * (dot(value, dr, 1, 1) - delta_row)
                ps[c, :, t * 256 : (t + 1) * 256] = p.astype(BF16)
                dss[c, :, t * 256 : (t + 1) * 256] = g.astype(BF16)
        q_all = q_s[a, src].reshape(1024, FEAT)
        do_all = do_s[a, src].reshape(1024, FEAT)
        for c, j in enumerate(chunks):
            dk = dot(dss[c], q_all, 1, 0)
            dv = dot(ps[c], do_all, 1, 0)
            if add:
                dkv[a, j, 0] += dk
                dkv[a, j, 1] += dv
            else:
                dkv[a, j, 0] = dk
                dkv[a, j, 1] = dv
        dq_t[a, src] += dot(kv_s[a, chunks[0], 0], dss[0], 0, 0) + dot(kv_s[a, chunks[1], 0], dss[1], 0, 0)

    for a in range(2):
        for t, ref in enumerate((q_s, do_s)):
            pltpu.make_async_copy(ref.at[a, y], ref.at[a, y], sem_ql.at[a, t]).wait()

    def own_step(i, carry):
        s, a = i // 2, i % 2
        for d in range(2):
            steps = jnp.where(a == d, 4, 3)

            @pl.when(s < steps)
            def _():
                gather_wait(d, a, s)

            @pl.when(s + 1 < steps)
            def _():
                gather_copy(d, a, s + 1).start()

        pair_unit(a, y, s, False)
        return carry

    lax.fori_loop(0, 8, own_step, 0)

    def reduce_copy(d, a, s):
        return remote(
            rs_out.at[d, a, s], rs_in.at[d, a, s], sem_rs.at[d, a, s], sem_rr.at[d, a, s], ring[d]
        )

    def reduce_step(d, a, s):
        left = jnp.where(a == d, 4, 3) - s
        j = (z + left) % 8 if d == 0 else (z + 8 - left) % 8

        @pl.when(s == 0)
        def _():
            rs_out[d, a, 0] = dkv[a, j].astype(BF16)

        @pl.when(s > 0)
        def _():
            before_s = jnp.maximum(s - 1, 0)
            reduce_copy(d, a, before_s).wait_recv()
            rs_out[d, a, s] = (dkv[a, j] + rs_in[d, a, before_s].astype(F32)).astype(BF16)

        reduce_copy(d, a, s).start()

    st_send.wait_recv()

    def dq_send(a):
        return remote(dq_out.at[a], dq_in.at[a], sem_dqs.at[a], sem_dqr.at[a], partner)

    def dq_cols(who, a):
        return dq_hbm.at[:, span((2 * who + a) * 1024, 1024)]

    def partner_step(i, carry):
        a, p = i // 4, i % 4

        @pl.when(p == 0)
        def _():
            for t, ref in enumerate((q_s, do_s)):
                pltpu.make_async_copy(ref.at[a, yo], ref.at[a, yo], sem_qr.at[a, t]).wait()

        pair_unit(a, yo, 3 - p, True)

        @pl.when(p == 0)
        def _():
            @pl.when(a == 0)
            def _():
                reduce_step(0, 0, jnp.int32(0))

            @pl.when(a == 1)
            def _():
                reduce_step(1, 1, jnp.int32(0))

        @pl.when(p == 1)
        def _():
            @pl.when(a == 0)
            def _():
                reduce_step(1, 0, jnp.int32(0))

            @pl.when(a == 1)
            def _():
                reduce_step(0, 1, jnp.int32(0))

        @pl.when(jnp.logical_and(a == 1, p < 3))
        def _():
            reduce_step(0, 0, p + 1)

            @pl.when(p < 2)
            def _():
                reduce_step(1, 0, p + 1)

        @pl.when(p == 3)
        def _():
            for h in range(8):
                dq_out[a, h] = (dq_t[a, yo, :, h * FEAT : (h + 1) * FEAT].T * SCALE).astype(BF16)
            dq_send(a).start()

        return carry

    lax.fori_loop(0, 8, partner_step, 0)

    for a in range(2):
        for h in range(8):
            dq_stage[0, a, :, h * FEAT : (h + 1) * FEAT] = dq_t[a, y, :, h * FEAT : (h + 1) * FEAT].T * SCALE
        pltpu.make_async_copy(dq_stage.at[0, a], dq_cols(y, a), sem_out.at[0, a]).start()

    def late_step(s, carry):
        @pl.when(s < 3)
        def _():
            reduce_step(0, 1, s)

        reduce_step(1, 1, s)
        return carry

    lax.fori_loop(1, 4, late_step, 0)

    bh = jnp.where(first_half, b, prv)

    def finish(a):
        reduce_copy(0, a, 3 - a).wait_recv()
        reduce_copy(1, a, 2 + a).wait_recv()
        for kv, (ref, factor) in enumerate(((dk_hbm, SCALE), (dv_hbm, 1.0))):
            total = dkv[a, z, kv] + rs_in[0, a, 3 - a, kv].astype(F32) + rs_in[1, a, 2 + a, kv].astype(F32)
            fin[a, kv] = total * factor
            dst = ref.at[:, span((2 * y + a) * FEAT, FEAT)]
            far = fin.at[a, kv, span(yo * FEAT, FEAT)]
            near = fin.at[a, kv, span(y * FEAT, FEAT)]
            remote(far, dst, sem_fs.at[0, a, kv], sem_fr.at[y, a, kv], (bh, 2 * z + yo)).start()

            @pl.when(first_half)
            def _():
                pltpu.make_async_copy(near, dst, sem_fr.at[y, a, kv]).start()

            @pl.when(jnp.logical_not(first_half))
            def _():
                remote(near, dst, sem_fs.at[1, a, kv], sem_fr.at[y, a, kv], (bh, hd)).start()

    finish(0)
    finish(1)

    for a in range(2):
        dq_send(a).wait_recv()
        for h in range(8):
            dq_stage[1, a, :, h * FEAT : (h + 1) * FEAT] = dq_in[a, h].astype(F32)
        pltpu.make_async_copy(dq_stage.at[1, a], dq_cols(yo, a), sem_out.at[1, a]).start()

    for a in range(2):
        for t, ref in enumerate((q_s, do_s)):
            pltpu.make_async_copy(ref.at[a, y], ref.at[a, y], sem_qs.at[a, t]).wait()
        for kv in range(2):
            half = kv_s.at[a, 0, kv, 0:FEAT]
            whole = fin.at[a, kv, 0:FEAT]
            pltpu.make_async_copy(half, half, sem_as.at[0, a, kv]).wait()
            pltpu.make_async_copy(whole, whole, sem_fs.at[0, a, kv]).wait()

            @pl.when(jnp.logical_not(first_half))
            def _():
                pltpu.make_async_copy(half, half, sem_as.at[1, a, kv]).wait()
                pltpu.make_async_copy(whole, whole, sem_fs.at[1, a, kv]).wait()

            for who in range(2):
                pltpu.make_async_copy(whole, whole, sem_fr.at[who, a, kv]).wait()
        for d in range(2):
            for s in range(4 if d == a else 3):
                gather_copy(d, a, s).wait_send()
                reduce_copy(d, a, s).wait_send()
        dq_send(a).wait_send()
        for who, device in enumerate((y, yo)):
            pltpu.make_async_copy(dq_stage.at[who, a], dq_cols(device, a), sem_out.at[who, a]).wait()
    st_send.wait_send()


def core(queries, key_matrix, value_matrix, saved_output, output_gradient, saved_logsumexp, block_order):
    dma = pltpu.SemaphoreType.DMA
    vmem = pltpu.VMEM
    anywhere = pl.BlockSpec(memory_space=pl.ANY)
    return pl.pallas_call(
        kernel,
        out_shape=[
            jax.ShapeDtypeStruct(queries.shape, F32),
            jax.ShapeDtypeStruct(key_matrix.shape, F32),
            jax.ShapeDtypeStruct(value_matrix.shape, F32),
        ],
        in_specs=[pl.BlockSpec(memory_space=pltpu.SMEM)]
        + [anywhere] * 5
        + [pl.BlockSpec(memory_space=pltpu.VMEM)],
        out_specs=[anywhere] * 3,
        scratch_shapes=[
            vmem((2, 2, 8, 128, 128), BF16),
            vmem((2, 2, 8, 128, 128), BF16),
            vmem((2, 8, 2, 256, 128), BF16),
            vmem((128, 4096), BF16),
            vmem((128, 4096), BF16),
            vmem((2, 32, 128), F32),
            vmem((2, 2, 16, 128), F32),
            vmem((128, 128), F32),
            vmem((3, 256, 256), F32),
            vmem((2, 256, 1024), BF16),
            vmem((2, 256, 1024), BF16),
            vmem((2, 2, 128, 1024), F32),
            vmem((2, 8, 2, 256, 128), F32),
            vmem((2, 2, 4, 2, 256, 128), BF16),
            vmem((2, 2, 4, 2, 256, 128), BF16),
            vmem((2, 2, 256, 128), F32),
            vmem((2, 8, 128, 128), BF16),
            vmem((2, 8, 128, 128), BF16),
            vmem((2, 2, 128, 1024), F32),
            dma((2,)),
            dma((2, 2)),
            dma((2, 2)),
            dma((2, 2)),
            dma((2,)),
            dma((2, 2, 2)),
            dma((2, 2, 2)),
            dma((2, 2, 4)),
            dma((2, 2, 4)),
            dma((2, 2, 4)),
            dma((2, 2, 4)),
            dma((2, 2, 2)),
            dma((2, 2, 2)),
            dma((2,)),
            dma((2,)),
            dma((2, 2)),
        ],
        compiler_params=pltpu.CompilerParams(
            collective_id=0, has_side_effects=True, vmem_limit_bytes=48 << 20
        ),
        name="attention_backward",
    )(
        block_order, queries, key_matrix, value_matrix, saved_output, output_gradient, saved_logsumexp
    )


def solution(mesh):
    rows = P(("blk", "head"), None)
    return jax.shard_map(
        core,
        mesh=mesh,
        in_specs=(rows,) * 6 + (P(),),
        out_specs=(rows,) * 3,
        check_vma=False,
    )
```

time: 358 us -> 88.9 us (0.25)
  the two profiles are of different devices: /device:TPU:7 before, /device:TPU:8 now
where the time goes in v1:
time: 88.9 us; the launch traced here: 87.9 us
  Pallas kernels  77.5 us (87%)
  local copies, waits for them, and re-layouts  9.67 us (11%)
    pallas_call x1, Pallas kernels, core(): pl.pallas_call(kernel, out_shape=[jax.ShapeDtypeStruct(queries.shape, F32...  77.5 us
    unnamed x16, local copies, waits for them, and re-layouts  9.67 us

profile of v1, /device:TPU:8, one launch (start us, length us, event | category | flops | bytes accessed | tf_op | source)
XLA Modules:
  0.0 87.9 jit_solution(767764884759582617)
XLA Ops:
  0.6 0.8 copy.10.lse_ref
  1.4 0.0 copy-start
  1.5 1.2 %copy-done = bf16[128,4096]{1,0:T(8,128)(2,1)S(1)} copy-done((bf16[128,4096]{1,0:T(8,128)(2,1)S(1)}, bf16[128,4096]{1,0:T(8,128)(2,1)}, u32[]{:S(2)}) %copy-start) | copy-done | bytes 1048600
  2.7 0.0 copy-start.1
  2.7 1.2 %copy-done.1 = bf16[128,4096]{1,0:T(8,128)(2,1)S(1)} copy-done((bf16[128,4096]{1,0:T(8,128)(2,1)S(1)}, bf16[128,4096]{1,0:T(8,128)(2,1)}, u32[]{:S(2)}) %copy-start.1) | copy-done | bytes 1048600
  3.9 0.0 copy-start.2
  3.9 1.2 %copy-done.2 = bf16[128,4096]{1,0:T(8,128)(2,1)S(1)} copy-done((bf16[128,4096]{1,0:T(8,128)(2,1)S(1)}, bf16[128,4096]{1,0:T(8,128)(2,1)}, u32[]{:S(2)}) %copy-start.2) | copy-done | bytes 1048600
  5.1 0.0 copy-start.3
  5.1 0.9 %copy-done.3 = bf16[128,512]{1,0:T(8,128)(2,1)S(1)} copy-done((bf16[128,512]{1,0:T(8,128)(2,1)S(1)}, bf16[128,512]{1,0:T(8,128)(2,1)}, u32[]{:S(2)}) %copy-start.3) | copy-done | bytes 131096
  6.0 0.0 copy-start.4
  6.0 0.9 %copy-done.4 = bf16[128,512]{1,0:T(8,128)(2,1)S(1)} copy-done((bf16[128,512]{1,0:T(8,128)(2,1)S(1)}, bf16[128,512]{1,0:T(8,128)(2,1)}, u32[]{:S(2)}) %copy-start.4) | copy-done | bytes 131096
  6.9 0.0 copy-start.5
  6.9 0.7 copy-done.5
  7.6 77.5 %attention_backward.1 = (f32[128,4096]{1,0:T(8,128)S(1)}, f32[128,512]{1,0:T(8,128)S(1)}, f32[128,512]{1,0:T(8,128)S(1)}) custom-call(s32[32]{0:T(128)S(1)} %copy-done.5, bf16[128,4096]{1,0:T(8,128)(2,1)S(1)} %copy-done, bf16[128,512]{1,0:T(8,128)(2,1)S(1)} %copy-done.3, bf16[128,512]{1,0:T(8,128)(2,1)S(1)} %copy-done.4, bf16[128,4096]{1,0:T(8,128)(2,1)S(1)} %copy-done.1, ...), custom_call_target="tpu_custom_call" | custom-call | tf_op jit(solution)/shard_map/attention_backward/pallas_call | solution.py:359
  85.1 1.3 %copy.14 = f32[128,4096]{1,0:T(8,128)} copy(f32[128,4096]{1,0:T(8,128)S(1)} %get-tuple-element.6) | data formatting | bytes 4194304
  86.5 0.7 copy.15
  87.2 0.7 copy.16
Async XLA Ops:
  1.4 1.2 %copy-start = (bf16[128,4096]{1,0:T(8,128)(2,1)S(1)}, bf16[128,4096]{1,0:T(8,128)(2,1)}, u32[]{:S(2)}) copy-start(bf16[128,4096]{1,0:T(8,128)(2,1)} %q_hbm.1) | copy-start | bytes 3145732
  2.7 1.2 %copy-start.1 = (bf16[128,4096]{1,0:T(8,128)(2,1)S(1)}, bf16[128,4096]{1,0:T(8,128)(2,1)}, u32[]{:S(2)}) copy-start(bf16[128,4096]{1,0:T(8,128)(2,1)} %o_hbm.1) | copy-start | bytes 3145732
  3.9 1.2 %copy-start.2 = (bf16[128,4096]{1,0:T(8,128)(2,1)S(1)}, bf16[128,4096]{1,0:T(8,128)(2,1)}, u32[]{:S(2)}) copy-start(bf16[128,4096]{1,0:T(8,128)(2,1)} %do_hbm.1) | copy-start | bytes 3145732
  5.1 0.9 %copy-start.3 = (bf16[128,512]{1,0:T(8,128)(2,1)S(1)}, bf16[128,512]{1,0:T(8,128)(2,1)}, u32[]{:S(2)}) copy-start(bf16[128,512]{1,0:T(8,128)(2,1)} %k_hbm.1) | copy-start | bytes 393220
  6.0 0.9 %copy-start.4 = (bf16[128,512]{1,0:T(8,128)(2,1)S(1)}, bf16[128,512]{1,0:T(8,128)(2,1)}, u32[]{:S(2)}) copy-start(bf16[128,512]{1,0:T(8,128)(2,1)} %v_hbm.1) | copy-start | bytes 393220
  6.9 0.7 copy-start.5

commit v2 on v1

v2 whole, which is shorter than its diff:
```python
import functools

import jax
import jax.numpy as jnp
from jax import lax
from jax.experimental import pallas as pl
from jax.experimental.pallas import tpu as pltpu
from jax.sharding import PartitionSpec as P

F32 = jnp.float32
BF16 = jnp.bfloat16
FEAT = 128
SCALE = FEAT**-0.5
LOG2E = 1.4426950408889634
UNSEEN = 1e30
MESH = pl.DeviceIdType.MESH

UNITS = (
    ((0, -1), (0, 1), False),
    ((1, -1), (1, 1), False),
    ((0, -2), (0, 2), False),
    ((1, -2), (1, 2), False),
    ((0, -1), (0, 1), True),
    ((0, -2), (0, 2), True),
    ((0, -3), (0, 3), False),
    ((0, -3), (0, 3), True),
    ((0, 4), (1, -3), False),
    ((0, 4), (0, 0), True),
    ((1, 3), (1, 4), False),
    ((1, 4), (1, 0), True),
    ((1, -3), (1, 3), True),
    ((1, -2), (1, 2), True),
    ((1, -1), (1, 1), True),
)


def dot(a, b, ca, cb):
    return lax.dot_general(a, b, (((ca,), (cb,)), ((), ())), preferred_element_type=F32)


def pick(n, values):
    out = jnp.int32(values[-1])
    for i, value in enumerate(values[:-1]):
        out = jnp.where(n == i, value, out)
    return out


def span(start, size):
    return pl.ds(pl.multiple_of(start, size), size)


def kernel(
    order_hbm, q_hbm, k_hbm, v_hbm, o_hbm, do_hbm, lse_hbm, dq_hbm, dk_hbm, dv_hbm,
    order, q_s, do_s, kv_s, o_full, do_full, lse_s, st_own, st_s, mask_s, ps, dss, dq_t, dkv,
    rs_in, rs_out, fin, dq_out, dq_in, dq_stage,
    sem_full, sem_ql, sem_qr, sem_qs, sem_st, sem_ar, sem_as, sem_gr, sem_gs, sem_rr, sem_rs,
    sem_fr, sem_fs, sem_dqr, sem_dqs, sem_out,
):
    b = lax.axis_index("blk")
    hd = lax.axis_index("head")
    z = hd // 2
    y = hd % 2
    yo = 1 - y
    partner = (b, 2 * z + yo)
    ring = ((b, (hd + 2) % 16), (b, (hd + 14) % 16))
    nxt = (b + 1) % 16
    prv = (b + 15) % 16
    first_half = z < 4
    later_half = jnp.logical_not(first_half)

    barrier = pltpu.get_barrier_semaphore()
    up, down = (hd + 2) % 16, (hd + 14) % 16
    peers = [partner, ring[0], ring[1]]
    peers += [(other, at) for other in (nxt, prv) for at in (hd, 2 * z + yo, up, down)]
    for peer in peers:
        pl.semaphore_signal(barrier, inc=1, device_id=peer, device_id_type=MESH)

    loads = [
        pltpu.make_async_copy(src, dst, sem_full.at[i])
        for i, (src, dst) in enumerate(
            ((o_hbm, o_full), (do_hbm, do_full), (lse_hbm, lse_s), (order_hbm, order))
        )
    ]
    for load in loads:
        load.start()

    def local_part(a, kv):
        ref = (k_hbm, v_hbm)[kv]
        return pltpu.make_async_copy(
            ref.at[:, span((2 * y + a) * FEAT, FEAT)], kv_s.at[a, z, y, kv], sem_ar.at[a, kv, y]
        )

    @pl.when(first_half)
    def _():
        for a in range(2):
            for kv in range(2):
                local_part(a, kv).start()

    for a in range(2):
        for t, (src, dst) in enumerate(((q_hbm, q_s), (do_hbm, do_s))):

            def one(h, c):
                pltpu.make_async_copy(
                    src.at[:, span((16 * y + 8 * a + h) * FEAT, FEAT)], dst.at[a, y, h], sem_ql.at[a, t]
                ).start()
                return c

            lax.fori_loop(0, 8, one, 0)

    dkv[...] = jnp.zeros_like(dkv)
    dq_t[...] = jnp.zeros_like(dq_t)
    key_row = lax.broadcasted_iota(jnp.int32, (256, 256), 0)
    query_row = lax.broadcasted_iota(jnp.int32, (256, 256), 1) % FEAT
    mask_s[0] = jnp.zeros((256, 256), F32)
    for slot in range(2):
        mask_s[1 + slot] = jnp.where(key_row > slot * FEAT + query_row, UNSEEN, 0.0)

    pl.semaphore_wait(barrier, len(peers))

    def remote(src, dst, ss, rs, dev):
        return pltpu.make_async_remote_copy(
            src_ref=src, dst_ref=dst, send_sem=ss, recv_sem=rs, device_id=dev, device_id_type=MESH
        )

    bt = jnp.where(first_half, b, nxt)
    for a in range(2):
        for kv, ref in enumerate((k_hbm, v_hbm)):
            near = ref.at[:, span((2 * y + a) * FEAT, FEAT)]
            dst = kv_s.at[a, z, y, kv]
            for d, at in enumerate((up, down)):
                remote(near, dst, sem_gs.at[d, a, 0, y], sem_gr.at[d, a, 0, y], (bt, at)).start()
    for a in range(2):
        for kv, ref in enumerate((k_hbm, v_hbm)):
            far = ref.at[:, span((2 * yo + a) * FEAT, FEAT)]
            remote(
                far, kv_s.at[a, z, y, kv], sem_as.at[0, a, kv], sem_ar.at[a, kv, y], (bt, 2 * z + yo)
            ).start()
    for a in range(2):
        for kv, ref in enumerate((k_hbm, v_hbm)):
            near = ref.at[:, span((2 * y + a) * FEAT, FEAT)]

            @pl.when(later_half)
            def _():
                remote(
                    near, kv_s.at[a, z, y, kv], sem_as.at[1, a, kv], sem_ar.at[a, kv, y], (bt, hd)
                ).start()

    def q_part(g):
        a, quad, t = g // 4, (g // 2) % 2, g % 2
        return a, quad, t, ((q_hbm, q_s), (do_hbm, do_s))[t]

    def q_send(g):
        a, quad, t, (src, dst) = q_part(g)

        def one(h, c):
            remote(
                src.at[:, span((16 * yo + 8 * a + h) * FEAT, FEAT)], dst.at[a, y, h],
                sem_qs.at[a, t, quad], sem_qr.at[a, t, quad], partner,
            ).start()
            return c

        lax.fori_loop(4 * quad, 4 * quad + 4, one, 0)

    def q_sent(g):
        a, quad, t, (_, dst) = q_part(g)
        place = dst.at[a, y, pl.ds(4 * quad, 4)]
        pltpu.make_async_copy(place, place, sem_qs.at[a, t, quad]).wait()

    def q_next(g):
        q_sent(g)
        q_send(g + 2)

    def gather_copy(d, a, s, half):
        j = (z + 8 - s) % 8 if d == 0 else (z + s) % 8
        piece = kv_s.at[a, j, half]
        return remote(piece, piece, sem_gs.at[d, a, s, half], sem_gr.at[d, a, s, half], ring[d])

    def own_chunk(a, half):
        for kv in range(2):
            place = kv_s.at[a, z, half, kv]
            pltpu.make_async_copy(place, place, sem_ar.at[a, kv, half]).wait()

    def gather_on(slot):
        s, a, half = slot // 4, slot % 2, (y if slot % 4 < 2 else yo)
        for d in range(2):
            steps = 4 if a == d else 3
            if s < steps:
                gather_copy(d, a, s, half).wait_recv()
            if s + 1 < steps:
                gather_copy(d, a, s + 1, half).start()

    q_send(0)
    q_send(1)

    for load in loads:
        load.wait()
    lane = lax.broadcasted_iota(jnp.int32, (FEAT, FEAT), 1)
    stats = jnp.zeros((FEAT, FEAT), F32)
    for h in range(32):
        cols = slice(h * FEAT, (h + 1) * FEAT)
        product = o_full[:, cols].astype(F32) * do_full[:, cols].astype(F32)
        stats = jnp.where(lane == h, jnp.sum(product, axis=1, keepdims=True), stats)
    st_own[0] = lse_s[...] * LOG2E
    st_own[1] = stats.T[0:32]
    st_send = remote(
        st_own.at[:, span(16 * yo, 16)], st_s.at[y], sem_st.at[0], sem_st.at[1], partner
    )
    st_send.start()
    st_s[y] = st_own[:, span(16 * y, 16)]

    for a in range(2):
        own_chunk(a, yo)
        for d in range(2):
            gather_copy(d, a, 0, yo).start()
    for a in range(2):
        own_chunk(a, y)

    own_a, own_b, before = order[2 * b], order[2 * b + 1], order[(2 * b + 31) % 32]
    query_seg = jnp.where(first_half, own_a, own_b)

    def penalty(j):
        inside = jnp.where(first_half, jnp.where(j <= z, 0.0, UNSEEN), jnp.where(own_b > own_a, 0.0, UNSEEN))
        return jnp.where(j >= 4, jnp.where(query_seg > before, 0.0, UNSEEN), inside)

    def pair_unit(src, chunks, masks):
        for c, (a, j) in enumerate(chunks):
            key = kv_s[a, j, :, 0].reshape(256, FEAT)
            value = kv_s[a, j, :, 1].reshape(256, FEAT)
            pen = penalty(j)
            for t in range(4):
                qr = q_s[a, src, 2 * t : 2 * t + 2].reshape(256, FEAT)
                dr = do_s[a, src, 2 * t : 2 * t + 2].reshape(256, FEAT)
                rows = [st_s[src, k, pl.ds(8 * a + 2 * t + i, 1)] for k in range(2) for i in range(2)]
                lse_row = jnp.concatenate(rows[0:2], axis=1) + pen
                delta_row = jnp.concatenate(rows[2:4], axis=1)
                x = dot(key, qr, 1, 1) * (SCALE * LOG2E) - lse_row
                if masks[c] is not None:
                    x = x - mask_s[masks[c]]
                p = jnp.exp2(x)
                g = p * (dot(value, dr, 1, 1) - delta_row)
                ps[c, :, t * 256 : (t + 1) * 256] = p.astype(BF16)
                dss[c, :, t * 256 : (t + 1) * 256] = g.astype(BF16)
        for c, (a, j) in enumerate(chunks):
            dkv[a, j, 0] += dot(dss[c], q_s[a, src].reshape(1024, FEAT), 1, 0)
            dkv[a, j, 1] += dot(ps[c], do_s[a, src].reshape(1024, FEAT), 1, 0)
            dq_t[a, src] += dot(kv_s[a, j, :, 0].reshape(256, FEAT), dss[c], 0, 0)

    for a in range(2):
        for t, ref in enumerate((q_s, do_s)):
            pltpu.make_async_copy(ref.at[a, y], ref.at[a, y], sem_ql.at[a, t]).wait()
    diagonal = jnp.where(first_half, 1 + y, 0)
    pair_unit(y, ((0, z), (1, z)), (diagonal, diagonal))

    def reduce_copy(d, a, s, kv):
        return remote(
            rs_out.at[d, a, s, kv], rs_in.at[d, a, s, kv], sem_rs.at[d, a, s, kv], sem_rr.at[d, a, s, kv], ring[d]
        )

    def reduce_step(d, a, s):
        left = (4 if a == d else 3) - s
        j = (z + left) % 8 if d == 0 else (z + 8 - left) % 8
        for kv in (1, 0):
            part = dkv[a, j, kv]
            if s > 0:
                reduce_copy(d, a, s - 1, kv).wait_recv()
                part = part + rs_in[d, a, s - 1, kv].astype(F32)
            rs_out[d, a, s, kv] = part.astype(BF16)
            reduce_copy(d, a, s, kv).start()

    def dq_send(a):
        return remote(dq_out.at[a], dq_in.at[a], sem_dqs.at[a], sem_dqr.at[a], partner)

    def dq_cols(who, a):
        return dq_hbm.at[:, span((2 * who + a) * 1024, 1024)]

    def dq_away(a):
        for h in range(8):
            dq_out[a, h] = (dq_t[a, yo, :, h * FEAT : (h + 1) * FEAT].T * SCALE).astype(BF16)
        dq_send(a).start()

    def dq_keep(a):
        for h in range(8):
            dq_stage[0, a, :, h * FEAT : (h + 1) * FEAT] = dq_t[a, y, :, h * FEAT : (h + 1) * FEAT].T * SCALE
        pltpu.make_async_copy(dq_stage.at[0, a], dq_cols(y, a), sem_out.at[0, a]).start()

    def dq_back(a):
        dq_send(a).wait_recv()
        for h in range(8):
            dq_stage[1, a, :, h * FEAT : (h + 1) * FEAT] = dq_in[a, h].astype(F32)
        pltpu.make_async_copy(dq_stage.at[1, a], dq_cols(yo, a), sem_out.at[1, a]).start()

    def partner_rows(a):
        for g in range(4 * a, 4 * a + 4):
            _, quad, t, (_, dst) = q_part(g)
            place = dst.at[a, yo, pl.ds(4 * quad, 4)]
            pltpu.make_async_copy(place, place, sem_qr.at[a, t, quad]).wait()

    bh = jnp.where(first_half, b, prv)

    def finish(a):
        for kv, (ref, factor) in ((1, (dv_hbm, 1.0)), (0, (dk_hbm, SCALE))):
            reduce_copy(0, a, 3 - a, kv).wait_recv()
            reduce_copy(1, a, 2 + a, kv).wait_recv()
            total = dkv[a, z, kv] + rs_in[0, a, 3 - a, kv].astype(F32) + rs_in[1, a, 2 + a, kv].astype(F32)
            fin[a, kv] = total * factor
            dst = ref.at[:, span((2 * y + a) * FEAT, FEAT)]
            far = fin.at[a, kv, span(yo * FEAT, FEAT)]
            near = fin.at[a, kv, span(y * FEAT, FEAT)]
            remote(far, dst, sem_fs.at[0, a, kv], sem_fr.at[y, a, kv], (bh, 2 * z + yo)).start()

            @pl.when(first_half)
            def _():
                pltpu.make_async_copy(near, dst, sem_fr.at[y, a, kv]).start()

            @pl.when(later_half)
            def _():
                remote(near, dst, sem_fs.at[1, a, kv], sem_fr.at[y, a, kv], (bh, hd)).start()

    before_unit = {
        0: lambda: (gather_on(0), gather_on(1), gather_on(2)),
        1: lambda: (gather_on(3), q_next(0)),
        2: lambda: (gather_on(4), q_next(1), gather_on(5), gather_on(6)),
        3: lambda: (gather_on(7), q_next(2)),
        4: lambda: (gather_on(8), q_next(3), st_send.wait_recv(), partner_rows(0)),
        5: lambda: gather_on(9),
        6: lambda: (gather_on(10), q_next(4)),
        7: lambda: gather_on(11),
        8: lambda: (q_next(5), gather_on(12), gather_on(13), gather_on(14)),
        10: lambda: gather_on(15),
        11: lambda: partner_rows(1),
    }
    after_unit = {
        7: lambda: reduce_step(1, 0, 0),
        9: lambda: (reduce_step(0, 0, 0), dq_away(0)),
        10: lambda: reduce_step(1, 0, 1),
        11: lambda: reduce_step(1, 1, 0),
        12: lambda: (reduce_step(0, 1, 0), reduce_step(0, 0, 1)),
        13: lambda: reduce_step(1, 0, 2),
        14: lambda: (dq_away(1), reduce_step(1, 1, 1), reduce_step(0, 1, 1), reduce_step(0, 0, 2)),
    }

    def unit_step(n, carry):
        for at, action in before_unit.items():
            pl.when(n == at)(lambda action=action: (action(), None)[1])
        chunks = tuple(
            (pick(n, [u[c][0] for u in UNITS]), (z + 8 + pick(n, [u[c][1] for u in UNITS])) % 8)
            for c in range(2)
        )
        away = pick(n, [int(u[2]) for u in UNITS])
        src = jnp.where(away == 1, yo, y)
        masked = jnp.where(jnp.logical_and(chunks[1][1] == z, first_half), 1 + src, 0)
        pair_unit(src, chunks, (None, masked))
        for at, action in after_unit.items():
            pl.when(n == at)(lambda action=action: (action(), None)[1])
        return carry

    lax.fori_loop(0, len(UNITS), unit_step, 0)

    dq_keep(0)
    dq_keep(1)
    reduce_step(1, 1, 2)
    reduce_step(0, 1, 2)
    reduce_step(0, 0, 3)
    dq_back(0)
    reduce_step(1, 1, 3)
    finish(0)
    dq_back(1)
    finish(1)

    q_sent(6)
    q_sent(7)
    for a in range(2):
        for kv in range(2):
            half = kv_s.at[a, 0, 0, kv]
            whole = fin.at[a, kv, 0:FEAT]
            pltpu.make_async_copy(half, half, sem_as.at[0, a, kv]).wait()
            pltpu.make_async_copy(whole, whole, sem_fs.at[0, a, kv]).wait()

            @pl.when(later_half)
            def _():
                pltpu.make_async_copy(half, half, sem_as.at[1, a, kv]).wait()
                pltpu.make_async_copy(whole, whole, sem_fs.at[1, a, kv]).wait()

            for who in range(2):
                pltpu.make_async_copy(whole, whole, sem_fr.at[who, a, kv]).wait()
        for d in range(2):
            for s in range(4 if d == a else 3):
                for i in range(2):
                    gather_copy(d, a, s, i).wait_send()
                    reduce_copy(d, a, s, i).wait_send()
        dq_send(a).wait_send()
        for who, device in enumerate((y, yo)):
            pltpu.make_async_copy(dq_stage.at[who, a], dq_cols(device, a), sem_out.at[who, a]).wait()
    st_send.wait_send()


def settle(*refs):
    sources, results, held, sems = refs[0:3], refs[3:6], refs[6:9], refs[9]
    loads, stores = [], []
    for src, mid, dst, parts in zip(sources, held, results, (8, 2, 2)):
        rows = src.shape[0] // parts
        for i in range(parts):
            at = pl.ds(i * rows, rows)
            n = len(loads)
            loads.append(pltpu.make_async_copy(src.at[at], mid.at[at], sems.at[0, n]))
            stores.append(pltpu.make_async_copy(mid.at[at], dst.at[at], sems.at[1, n]))
    for load in loads:
        load.start()
    for load, store in zip(loads, stores):
        load.wait()
        store.start()
    for store in stores:
        store.wait()


def core(queries, key_matrix, value_matrix, saved_output, output_gradient, saved_logsumexp, block_order):
    dma = pltpu.SemaphoreType.DMA
    vmem = pltpu.VMEM
    hbm = pl.BlockSpec(memory_space=pltpu.HBM)
    shapes = [
        jax.ShapeDtypeStruct(array.shape, F32) for array in (queries, key_matrix, value_matrix)
    ]
    gradients = pl.pallas_call(
        kernel,
        out_shape=shapes,
        in_specs=[hbm] * 7,
        out_specs=[hbm] * 3,
        scratch_shapes=[
            pltpu.SMEM((32,), jnp.int32),
            vmem((2, 2, 8, 128, 128), BF16),
            vmem((2, 2, 8, 128, 128), BF16),
            vmem((2, 8, 2, 2, 128, 128), BF16),
            vmem((128, 4096), BF16),
            vmem((128, 4096), BF16),
            vmem((32, 128), F32),
            vmem((2, 32, 128), F32),
            vmem((2, 2, 16, 128), F32),
            vmem((3, 256, 256), F32),
            vmem((2, 256, 1024), BF16),
            vmem((2, 256, 1024), BF16),
            vmem((2, 2, 128, 1024), F32),
            vmem((2, 8, 2, 256, 128), F32),
            vmem((2, 2, 4, 2, 256, 128), BF16),
            vmem((2, 2, 4, 2, 256, 128), BF16),
            vmem((2, 2, 256, 128), F32),
            vmem((2, 8, 128, 128), BF16),
            vmem((2, 8, 128, 128), BF16),
            vmem((2, 2, 128, 1024), F32),
            dma((4,)),
            dma((2, 2)),
            dma((2, 2, 2)),
            dma((2, 2, 2)),
            dma((2,)),
            dma((2, 2, 2)),
            dma((2, 2, 2)),
            dma((2, 2, 4, 2)),
            dma((2, 2, 4, 2)),
            dma((2, 2, 4, 2)),
            dma((2, 2, 4, 2)),
            dma((2, 2, 2)),
            dma((2, 2, 2)),
            dma((2,)),
            dma((2,)),
            dma((2, 2)),
        ],
        compiler_params=pltpu.CompilerParams(
            collective_id=0, has_side_effects=True, vmem_limit_bytes=62 << 20
        ),
        name="attention_backward",
    )(
        block_order, queries, key_matrix, value_matrix, saved_output, output_gradient, saved_logsumexp.T
    )
    return pl.pallas_call(
        settle,
        out_shape=shapes,
        in_specs=[hbm] * 3,
        out_specs=[hbm] * 3,
        scratch_shapes=[vmem(shape.shape, F32) for shape in shapes] + [dma((2, 12))],
        compiler_params=pltpu.CompilerParams(vmem_limit_bytes=62 << 20),
        name="settle",
    )(*gradients)


def solution(mesh):
    rows = P(("blk", "head"), None)
    return jax.shard_map(
        core,
        mesh=mesh,
        in_specs=(rows,) * 6 + (P(),),
        out_specs=(rows,) * 3,
        check_vma=False,
    )
```

time: 88.9 us -> 72.6 us (0.82)
  local copies, waits for them, and re-layouts: 9.67 us -> 0 us
  Pallas kernels: 77.5 us -> 70.6 us
    unnamed x16 -> x0, local copies, waits for them, and re-layouts: 9.67 us -> none
    pallas_call x1 -> x2, Pallas kernels: 77.5 us -> 70.6 us  [the longest x1 67.9 us: core(): pl.pallas_call(kernel, out_shape=shapes, in_specs=[hbm] * 7, out_specs=[h...]
where the time goes in v2:
time: 72.6 us; the launch traced here: 71.2 us
  Pallas kernels  70.6 us (97%)
    pallas_call x1, Pallas kernels, core(): pl.pallas_call(kernel, out_shape=shapes, in_specs=[hbm] * 7, out_specs=[h...  67.9 us
    pallas_call x1, Pallas kernels, core(): pl.pallas_call(settle, out_shape=shapes, in_specs=[hbm] * 3, out_specs=[h...  2.63 us

profile of v2, /device:TPU:8, one launch (start us, length us, event | category | flops | bytes accessed | tf_op | source)
XLA Modules:
  0.0 71.2 jit_solution(3890017599692349851)
XLA Ops:
  0.6 67.9 %attention_backward.1 = (f32[128,4096]{1,0:T(8,128)}, f32[128,512]{1,0:T(8,128)}, f32[128,512]{1,0:T(8,128)}) custom-call(s32[32]{0:T(128)} %order_hbm.1, bf16[128,4096]{1,0:T(8,128)(2,1)} %q_hbm.1, bf16[128,512]{1,0:T(8,128)(2,1)} %k_hbm.1, bf16[128,512]{1,0:T(8,128)(2,1)} %v_hbm.1, bf16[128,4096]{1,0:T(8,128)(2,1)} %o_hbm.1, bf16[128,4096]{1,0:T(8,128)(2,1)} %do_hbm.1, ...), custom_call_target="tpu_custom_call" | custom-call | tf_op jit(solution)/shard_map/attention_backward/pallas_call | solution.py:423
  68.6 2.6 %settle.1 = (f32[128,4096]{1,0:T(8,128)}, f32[128,512]{1,0:T(8,128)}, f32[128,512]{1,0:T(8,128)}) custom-call(f32[128,4096]{1,0:T(8,128)} %get-tuple-element.6.refs_0_, f32[128,512]{1,0:T(8,128)} %get-tuple-element.7.refs_1_, f32[128,512]{1,0:T(8,128)} %get-tuple-element.8.refs_2_), custom_call_target="tpu_custom_call" | custom-call | tf_op jit(solution)/shard_map/settle/pallas_call | solution.py:473

commit v3 on v2

--- a/solution.py
+++ b/solution.py
@@ -52,9 +52,9 @@
 def kernel(
     order_hbm, q_hbm, k_hbm, v_hbm, o_hbm, do_hbm, lse_hbm, dq_hbm, dk_hbm, dv_hbm,
     order, q_s, do_s, kv_s, o_full, do_full, lse_s, st_own, st_s, mask_s, ps, dss, dq_t, dkv,
-    rs_in, rs_out, fin, dq_out, dq_in, dq_stage,
+    rs_in, rs_out, own_out, home_in, fin, dq_out, dq_in, dq_stage,
     sem_full, sem_ql, sem_qr, sem_qs, sem_st, sem_ar, sem_as, sem_gr, sem_gs, sem_rr, sem_rs,
-    sem_fr, sem_fs, sem_dqr, sem_dqs, sem_out,
+    sem_hr, sem_hs, sem_os, sem_fin, sem_dqr, sem_dqs, sem_out,
 ):
     b = lax.axis_index("blk")
     hd = lax.axis_index("head")
@@ -70,50 +70,12 @@
 
     barrier = pltpu.get_barrier_semaphore()
     up, down = (hd + 2) % 16, (hd + 14) % 16
-    peers = [partner, ring[0], ring[1]]
-    peers += [(other, at) for other in (nxt, prv) for at in (hd, 2 * z + yo, up, down)]
+    turn = yo - y
+    around = (2 * z + yo, up, down, up + turn, down + turn)
+    peers = [(b, at) for at in around]
+    peers += [(other, at) for other in (nxt, prv) for at in (hd,) + around]
     for peer in peers:
         pl.semaphore_signal(barrier, inc=1, device_id=peer, device_id_type=MESH)
-
-    loads = [
-        pltpu.make_async_copy(src, dst, sem_full.at[i])
-        for i, (src, dst) in enumerate(
-            ((o_hbm, o_full), (do_hbm, do_full), (lse_hbm, lse_s), (order_hbm, order))
-        )
-    ]
-    for load in loads:
-        load.start()
-
-    def local_part(a, kv):
-        ref = (k_hbm, v_hbm)[kv]
-        return pltpu.make_async_copy(
-            ref.at[:, span((2 * y + a) * FEAT, FEAT)], kv_s.at[a, z, y, kv], sem_ar.at[a, kv, y]
-        )
-
-    @pl.when(first_half)
-    def _():
-        for a in range(2):
-            for kv in range(2):
-                local_part(a, kv).start()
-
-    for a in range(2):
-        for t, (src, dst) in enumerate(((q_hbm, q_s), (do_hbm, do_s))):
-
-            def one(h, c):
-                pltpu.make_async_copy(
-                    src.at[:, span((16 * y + 8 * a + h) * FEAT, FEAT)], dst.at[a, y, h], sem_ql.at[a, t]
-                ).start()
-                return c
-
-            lax.fori_loop(0, 8, one, 0)
-
-    dkv[...] = jnp.zeros_like(dkv)
-    dq_t[...] = jnp.zeros_like(dq_t)
-    key_row = lax.broadcasted_iota(jnp.int32, (256, 256), 0)
-    query_row = lax.broadcasted_iota(jnp.int32, (256, 256), 1) % FEAT
-    mask_s[0] = jnp.zeros((256, 256), F32)
-    for slot in range(2):
-        mask_s[1 + slot] = jnp.where(key_row > slot * FEAT + query_row, UNSEEN, 0.0)
 
     pl.semaphore_wait(barrier, len(peers))
 
@@ -191,6 +153,46 @@
 
     q_send(0)
     q_send(1)
+
+    loads = [
+        pltpu.make_async_copy(src, dst, sem_full.at[i])
+        for i, (src, dst) in enumerate(
+            ((o_hbm, o_full), (do_hbm, do_full), (lse_hbm, lse_s), (order_hbm, order))
+        )
+    ]
+    for load in loads:
+        load.start()
+
+    def local_part(a, kv):
+        ref = (k_hbm, v_hbm)[kv]
+        return pltpu.make_async_copy(
+            ref.at[:, span((2 * y + a) * FEAT, FEAT)], kv_s.at[a, z, y, kv], sem_ar.at[a, kv, y]
+        )
+
+    @pl.when(first_half)
+    def _():
+        for a in range(2):
+            for kv in range(2):
+                local_part(a, kv).start()
+
+    for a in range(2):
+        for t, (src, dst) in enumerate(((q_hbm, q_s), (do_hbm, do_s))):
+
+            def one(h, c):
+                pltpu.make_async_copy(
+                    src.at[:, span((16 * y + 8 * a + h) * FEAT, FEAT)], dst.at[a, y, h], sem_ql.at[a, t]
+                ).start()
+                return c
+
+            lax.fori_loop(0, 8, one, 0)
+
+    dkv[...] = jnp.zeros_like(dkv)
+    dq_t[...] = jnp.zeros_like(dq_t)
+    key_row = lax.broadcasted_iota(jnp.int32, (256, 256), 0)
+    query_row = lax.broadcasted_iota(jnp.int32, (256, 256), 1) % FEAT
+    mask_s[0] = jnp.zeros((256, 256), F32)
+    for slot in range(2):
+        mask_s[1 + slot] = jnp.where(key_row > slot * FEAT + query_row, UNSEEN, 0.0)
 
     for load in loads:
         load.wait()
@@ -256,16 +258,48 @@
             rs_out.at[d, a, s, kv], rs_in.at[d, a, s, kv], sem_rs.at[d, a, s, kv], sem_rr.at[d, a, s, kv], ring[d]
         )
 
+    def home_copy(d, a, kv, half):
+        to_z = (z + 1) % 8 if d == 0 else (z + 7) % 8
+        device = (jnp.where(to_z < 4, b, prv), 2 * to_z + half)
+        return remote(
+            rs_out.at[d, a, 3 if d == a else 2, kv, half], home_in.at[y, d, a, kv],
+            sem_hs.at[d, a, kv, half], sem_hr.at[y, d, a, kv], device,
+        )
+
     def reduce_step(d, a, s):
-        left = (4 if a == d else 3) - s
+        steps = 4 if a == d else 3
+        left = steps - s
         j = (z + left) % 8 if d == 0 else (z + 8 - left) % 8
         for kv in (1, 0):
-            part = dkv[a, j, kv]
+            part = dkv[a, j, kv].reshape(2, FEAT, FEAT)
             if s > 0:
                 reduce_copy(d, a, s - 1, kv).wait_recv()
                 part = part + rs_in[d, a, s - 1, kv].astype(F32)
             rs_out[d, a, s, kv] = part.astype(BF16)
-            reduce_copy(d, a, s, kv).start()
+            if left > 1:
+                reduce_copy(d, a, s, kv).start()
+            else:
+                for half in range(2):
+                    home_copy(d, a, kv, half).start()
+
+    def own_copy(a, kv, half, device):
+        return remote(
+            own_out.at[a, kv, half], home_in.at[y, 2, a, kv], sem_os.at[a, kv, half], sem_hr.at[y, 2, a, kv], device
+        )
+
+    def own_send(a):
+        for kv in range(2):
+            for half in range(2):
+                own_out[a, kv, half] = dkv[a, z, kv, half * FEAT : (half + 1) * FEAT].astype(BF16)
+
+            @pl.when(first_half)
+            def _():
+                own_copy(a, kv, yo, (b, 2 * z + yo)).start()
+
+            @pl.when(later_half)
+            def _():
+                for half in range(2):
+                    own_copy(a, kv, half, (prv, 2 * z + half)).start()
 
     def dq_send(a):
         return remote(dq_out.at[a], dq_in.at[a], sem_dqs.at[a], sem_dqr.at[a], partner)
@@ -295,26 +329,28 @@
             place = dst.at[a, yo, pl.ds(4 * quad, 4)]
             pltpu.make_async_copy(place, place, sem_qr.at[a, t, quad]).wait()
 
-    bh = jnp.where(first_half, b, prv)
+    def landed(pair, part, a, kv):
+        place = home_in.at[pair, part, a, kv]
+        pltpu.make_async_copy(place, place, sem_hr.at[pair, part, a, kv]).wait()
+        return home_in[pair, part, a, kv].astype(F32)
 
     def finish(a):
         for kv, (ref, factor) in ((1, (dv_hbm, 1.0)), (0, (dk_hbm, SCALE))):
-            reduce_copy(0, a, 3 - a, kv).wait_recv()
-            reduce_copy(1, a, 2 + a, kv).wait_recv()
-            total = dkv[a, z, kv] + rs_in[0, a, 3 - a, kv].astype(F32) + rs_in[1, a, 2 + a, kv].astype(F32)
-            fin[a, kv] = total * factor
-            dst = ref.at[:, span((2 * y + a) * FEAT, FEAT)]
-            far = fin.at[a, kv, span(yo * FEAT, FEAT)]
-            near = fin.at[a, kv, span(y * FEAT, FEAT)]
-            remote(far, dst, sem_fs.at[0, a, kv], sem_fr.at[y, a, kv], (bh, 2 * z + yo)).start()
-
-            @pl.when(first_half)
-            def _():
-                pltpu.make_async_copy(near, dst, sem_fr.at[y, a, kv]).start()
-
-            @pl.when(later_half)
-            def _():
-                remote(near, dst, sem_fs.at[1, a, kv], sem_fr.at[y, a, kv], (bh, hd)).start()
+            for who, pair in enumerate((y, yo)):
+                total = landed(pair, 0, a, kv) + landed(pair, 1, a, kv)
+                mine = first_half if who == 0 else False
+
+                @pl.when(mine)
+                def _():
+                    fin[who, a, kv] = (total + dkv[a, z, kv, span(y * FEAT, FEAT)]) * factor
+
+                @pl.when(jnp.logical_not(mine))
+                def _():
+                    fin[who, a, kv] = (total + landed(pair, 2, a, kv)) * factor
+
+                pltpu.make_async_copy(
+                    fin.at[who, a, kv], ref.at[:, span((2 * pair + a) * FEAT, FEAT)], sem_fin.at[who, a, kv]
+                ).start()
 
     before_unit = {
         0: lambda: (gather_on(0), gather_on(1), gather_on(2)),
@@ -331,12 +367,12 @@
     }
     after_unit = {
         7: lambda: reduce_step(1, 0, 0),
-        9: lambda: (reduce_step(0, 0, 0), dq_away(0)),
-        10: lambda: reduce_step(1, 0, 1),
-        11: lambda: reduce_step(1, 1, 0),
-        12: lambda: (reduce_step(0, 1, 0), reduce_step(0, 0, 1)),
-        13: lambda: reduce_step(1, 0, 2),
-        14: lambda: (dq_away(1), reduce_step(1, 1, 1), reduce_step(0, 1, 1), reduce_step(0, 0, 2)),
+        9: lambda: (reduce_step(0, 0, 0), dq_away(0), own_send(0)),
+        10: lambda: (reduce_step(1, 0, 1), dq_keep(0), dq_keep(1)),
+        11: lambda: (reduce_step(1, 1, 0), reduce_step(0, 0, 1), own_send(1)),
+        12: lambda: (reduce_step(0, 1, 0), reduce_step(1, 0, 2)),
+        13: lambda: (reduce_step(1, 1, 1), reduce_step(0, 0, 2)),
+        14: lambda: (reduce_step(0, 1, 1), dq_away(1), reduce_step(1, 1, 2), reduce_step(0, 0, 3)),
     }
 
     def unit_step(n, carry):
@@ -356,13 +392,9 @@
 
     lax.fori_loop(0, len(UNITS), unit_step, 0)
 
-    dq_keep(0)
-    dq_keep(1)
-    reduce_step(1, 1, 2)
     reduce_step(0, 1, 2)
-    reduce_step(0, 0, 3)
+    reduce_step(1, 1, 3)
     dq_back(0)
-    reduce_step(1, 1, 3)
     finish(0)
     dq_back(1)
     finish(1)
@@ -371,23 +403,31 @@
     q_sent(7)
     for a in range(2):
         for kv in range(2):
-            half = kv_s.at[a, 0, 0, kv]
-            whole = fin.at[a, kv, 0:FEAT]
-            pltpu.make_async_copy(half, half, sem_as.at[0, a, kv]).wait()
-            pltpu.make_async_copy(whole, whole, sem_fs.at[0, a, kv]).wait()
+            place = kv_s.at[a, 0, 0, kv]
+            pltpu.make_async_copy(place, place, sem_as.at[0, a, kv]).wait()
+
+            @pl.when(first_half)
+            def _():
+                own_copy(a, kv, yo, partner).wait_send()
 
             @pl.when(later_half)
             def _():
-                pltpu.make_async_copy(half, half, sem_as.at[1, a, kv]).wait()
-                pltpu.make_async_copy(whole, whole, sem_fs.at[1, a, kv]).wait()
+                pltpu.make_async_copy(place, place, sem_as.at[1, a, kv]).wait()
+                for half in range(2):
+                    own_copy(a, kv, half, partner).wait_send()
 
             for who in range(2):
-                pltpu.make_async_copy(whole, whole, sem_fr.at[who, a, kv]).wait()
+                pltpu.make_async_copy(fin.at[who, a, kv], fin.at[who, a, kv], sem_fin.at[who, a, kv]).wait()
         for d in range(2):
-            for s in range(4 if d == a else 3):
-                for i in range(2):
-                    gather_copy(d, a, s, i).wait_send()
-                    reduce_copy(d, a, s, i).wait_send()
+            steps = 4 if d == a else 3
+            for half in range(2):
+                for s in range(steps):
+                    gather_copy(d, a, s, half).wait_send()
+                for kv in range(2):
+                    home_copy(d, a, kv, half).wait_send()
+            for kv in range(2):
+                for s in range(steps - 1):
+                    reduce_copy(d, a, s, kv).wait_send()
         dq_send(a).wait_send()
         for who, device in enumerate((y, yo)):
             pltpu.make_async_copy(dq_stage.at[who, a], dq_cols(device, a), sem_out.at[who, a]).wait()
@@ -440,9 +480,11 @@
             vmem((2, 256, 1024), BF16),
             vmem((2, 2, 128, 1024), F32),
             vmem((2, 8, 2, 256, 128), F32),
-            vmem((2, 2, 4, 2, 256, 128), BF16),
-            vmem((2, 2, 4, 2, 256, 128), BF16),
-            vmem((2, 2, 256, 128), F32),
+            vmem((2, 2, 3, 2, 2, 128, 128), BF16),
+            vmem((2, 2, 4, 2, 2, 128, 128), BF16),
+            vmem((2, 2, 2, 128, 128), BF16),
+            vmem((2, 3, 2, 2, 128, 128), BF16),
+            vmem((2, 2, 2, 128, 128), F32),
             vmem((2, 8, 128, 128), BF16),
             vmem((2, 8, 128, 128), BF16),
             vmem((2, 2, 128, 1024), F32),
@@ -455,8 +497,10 @@
             dma((2, 2, 2)),
             dma((2, 2, 4, 2)),
             dma((2, 2, 4, 2)),
-            dma((2, 2, 4, 2)),
-            dma((2, 2, 4, 2)),
+            dma((2, 2, 3, 2)),
+            dma((2, 2, 3, 2)),
+            dma((2, 3, 2, 2)),
+            dma((2, 2, 2, 2)),
             dma((2, 2, 2)),
             dma((2, 2, 2)),
             dma((2,)),

time: 72.6 us -> 67.8 us (0.934); the launches traced: 71.2 us -> 67.7 us
  Pallas kernels: 70.6 us -> 67 us
    pallas_call x1, Pallas kernels: 67.9 us -> 64.4 us  [core(): pl.pallas_call(kernel, out_shape=shapes, in_specs=[hbm] * 7, out_specs=[h...]
where the time goes in v3:
time: 67.8 us; the launch traced here: 67.7 us
  Pallas kernels  67 us (99%)
    pallas_call x1, Pallas kernels, core(): pl.pallas_call(kernel, out_shape=shapes, in_specs=[hbm] * 7, out_specs=[h...  64.4 us
    pallas_call x1, Pallas kernels, core(): pl.pallas_call(settle, out_shape=shapes, in_specs=[hbm] * 3, out_specs=[h...  2.63 us

profile of v3, /device:TPU:8, one launch (start us, length us, event | category | flops | bytes accessed | tf_op | source)
XLA Modules:
  0.0 67.7 jit_solution(10630162098253718995)
XLA Ops:
  0.6 64.4 %attention_backward.1 = (f32[128,4096]{1,0:T(8,128)}, f32[128,512]{1,0:T(8,128)}, f32[128,512]{1,0:T(8,128)}) custom-call(s32[32]{0:T(128)} %order_hbm.1, bf16[128,4096]{1,0:T(8,128)(2,1)} %q_hbm.1, bf16[128,512]{1,0:T(8,128)(2,1)} %k_hbm.1, bf16[128,512]{1,0:T(8,128)(2,1)} %v_hbm.1, bf16[128,4096]{1,0:T(8,128)(2,1)} %o_hbm.1, bf16[128,4096]{1,0:T(8,128)(2,1)} %do_hbm.1, ...), custom_call_target="tpu_custom_call" | custom-call | tf_op jit(solution)/shard_map/attention_backward/pallas_call | solution.py:463
  65.0 2.6 %settle.1 = (f32[128,4096]{1,0:T(8,128)}, f32[128,512]{1,0:T(8,128)}, f32[128,512]{1,0:T(8,128)}) custom-call(f32[128,4096]{1,0:T(8,128)} %get-tuple-element.6.refs_0_, f32[128,512]{1,0:T(8,128)} %get-tuple-element.7.refs_1_, f32[128,512]{1,0:T(8,128)} %get-tuple-element.8.refs_2_), custom_call_target="tpu_custom_call" | custom-call | tf_op jit(solution)/shard_map/settle/pallas_call | solution.py:517

commit v4 on v3

--- a/solution.py
+++ b/solution.py
@@ -74,7 +74,7 @@
     around = (2 * z + yo, up, down, up + turn, down + turn)
     peers = [(b, at) for at in around]
     peers += [(other, at) for other in (nxt, prv) for at in (hd,) + around]
-    for peer in peers:
+    for peer in reversed(peers):
         pl.semaphore_signal(barrier, inc=1, device_id=peer, device_id_type=MESH)
 
     pl.semaphore_wait(barrier, len(peers))

time: 67.8 us -> 67.7 us (level)
  no operation moved by 1% of the time
where the time goes in v4:
time: 67.7 us; the launch traced here: 67.6 us
  Pallas kernels  67 us (99%)
    pallas_call x1, Pallas kernels, core(): pl.pallas_call(kernel, out_shape=shapes, in_specs=[hbm] * 7, out_specs=[h...  64.3 us
    pallas_call x1, Pallas kernels, core(): pl.pallas_call(settle, out_shape=shapes, in_specs=[hbm] * 3, out_specs=[h...  2.63 us

profile of v4, /device:TPU:8, one launch (start us, length us, event | category | flops | bytes accessed | tf_op | source)
XLA Modules:
  0.0 67.6 jit_solution(8488529848036839294)
XLA Ops:
  0.6 64.3 %attention_backward.1 = (f32[128,4096]{1,0:T(8,128)}, f32[128,512]{1,0:T(8,128)}, f32[128,512]{1,0:T(8,128)}) custom-call(s32[32]{0:T(128)} %order_hbm.1, bf16[128,4096]{1,0:T(8,128)(2,1)} %q_hbm.1, bf16[128,512]{1,0:T(8,128)(2,1)} %k_hbm.1, bf16[128,512]{1,0:T(8,128)(2,1)} %v_hbm.1, bf16[128,4096]{1,0:T(8,128)(2,1)} %o_hbm.1, bf16[128,4096]{1,0:T(8,128)(2,1)} %do_hbm.1, ...), custom_call_target="tpu_custom_call" | custom-call | tf_op jit(solution)/shard_map/attention_backward/pallas_call | solution.py:463
  65.0 2.6 %settle.1 = (f32[128,4096]{1,0:T(8,128)}, f32[128,512]{1,0:T(8,128)}, f32[128,512]{1,0:T(8,128)}) custom-call(f32[128,4096]{1,0:T(8,128)} %get-tuple-element.6.refs_0_, f32[128,512]{1,0:T(8,128)} %get-tuple-element.7.refs_1_, f32[128,512]{1,0:T(8,128)} %get-tuple-element.8.refs_2_), custom_call_target="tpu_custom_call" | custom-call | tf_op jit(solution)/shard_map/settle/pallas_call | solution.py:517
